TPU v7x, 128 devices: a whole 4x4x4 slice. The times are simulated.
128 devices in a mesh: slab: 4 (over x), blk: 32 (over y, z, core).
Axes of the slice: x: 4, y: 4, z: 4, core: 2. Of those that a mesh axis runs over, the one named last changes fastest.
Arguments:
- populations: float32 [19, 128, 512, 128], P(None, 'slab', 'blk'), may hold values from 0.01 to 0.6, as said below
- solid: int32 [128, 512, 128], P('slab', 'blk'), may hold values 0 or 1
- wetting: int32 [128, 512, 128], P('slab', 'blk'), may hold values 0 or 1
- dest: int32 [4, 512], P('slab', 'blk'), may hold values from 0 to 511, as said below
Outputs:
- relocated: float32 [2048, 19, 4096], P(('slab', 'blk'))
Inputs may be any that keep to these rules, and one draw needn't show every extreme that they name: `populations`: every population is positive. dest[s, b * 16 + k] is the slot within slab group s that takes the k-th block of device b; every slot of a slab group appears once; dest[s, b * 16 + k] % 16 equals k; a device sends to any one owner, dest // 16, either none or exactly 1 of its blocks.
All inputs are finite; a program needn't handle non-finite values. No bound on the sum of `solid` or of `wetting` on one device may be relied on, other than what follows from the above.
Results may differ from a plain program's by a relative error of at most 0.0001.
Values sent between devices are 32-bit elements; how exact they have to be, the bound alone decides.
No kernel may reach another device: no remote copies, remote signals or barrier semaphores. Data moves between devices by JAX's collectives and lax.ppermute only.
A program may use at most 192 MiB of HBM per device.

v0:
```python
import functools

import jax
import jax.numpy as jnp
import numpy as np
from jax import lax
from jax.experimental import pallas as pl
from jax.experimental.pallas import tpu as pltpu
from jax.sharding import PartitionSpec as P

VELOCITIES = [
    (0, 0, 0), (1, 0, 0), (-1, 0, 0), (0, 1, 0), (0, -1, 0), (0, 0, 1), (0, 0, -1),
    (1, 1, 0), (-1, -1, 0), (1, -1, 0), (-1, 1, 0), (1, 0, 1), (-1, 0, -1), (1, 0, -1),
    (-1, 0, 1), (0, 1, 1), (0, -1, -1), (0, 1, -1), (0, -1, 1),
]
OPPOSITE = [0, 2, 1, 4, 3, 6, 5, 8, 7, 10, 9, 12, 11, 14, 13, 16, 15, 18, 17]
WEIGHTS = [1.0 / 3.0] + [1.0 / 18.0] * 6 + [1.0 / 36.0] * 12
WALL_DENSITY = 1.2
BIG = 1e30
HALF_BIG = 1e29

X_UP = [i for i in range(19) if VELOCITIES[i][0] == 1]
X_DOWN = [i for i in range(19) if VELOCITIES[i][0] == -1]
Y_UP = [i for i in range(19) if VELOCITIES[i][1] == 1]
Y_DOWN = [i for i in range(19) if VELOCITIES[i][1] == -1]

XS, YS, ZS = 32, 16, 128
HALO_ROWS = 40
CHUNK = 4
CHUNKS = XS // CHUNK
BLOCKS = 16
BLOCK_ROWS = 19 * 32
PITCH = 33


def collide(f):
    s, d = {}, {}
    for i in range(1, 19, 2):
        s[i] = f[i] + f[i + 1]
        d[i] = f[i] - f[i + 1]
    sxy, sxz, syz = s[7] + s[9], s[11] + s[13], s[15] + s[17]
    sx, sy, sz = s[1], s[3], s[5]
    rho = f[0] + (sx + sy) + (sz + sxy) + (sxz + syz)
    jx = d[1] + (d[7] + d[9]) + (d[11] + d[13])
    jy = d[3] + (d[7] - d[9]) + (d[15] + d[17])
    jz = d[5] + (d[11] - d[13]) + (d[15] - d[17])
    xx, yy, zz = jx * jx, jy * jy, jz * jz
    r = rho - 1.5 * (xx + yy + zz)
    tx, ty, tz = 2.0 * sx + 0.5 * xx, 2.0 * sy + 0.5 * yy, 2.0 * sz + 0.5 * zz
    base = 4.0 * f[0] - r
    qxy = (sxy - tx) + (base - ty + (xx + yy))
    qyz = (syz - ty) + (base - tz + (yy + zz))
    qxz = (sxz - tx) + (base - tz + (xx + zz))
    mean = (qxy + qyz + qxz) * (2.0 / 7.0)
    scale = 0.15 / 12.0
    a, b, c = (qxy - mean) * scale, (qyz - mean) * scale, (qxz - mean) * scale
    out = [None] * 19
    out[0] = -0.25 * f[0] + (1.25 / 3.0) * r - 4.0 * (a + b + c)
    axis_r = (1.25 / 18.0) * r
    plane_r = (1.25 / 36.0) * r

    def pair(i, along, square, even):
        w = WEIGHTS[i]
        e = even - 0.125 * s[i] + (1.25 * 4.5 * w) * square
        o = (1.6 * 3.0 * w) * along - 0.3 * d[i]
        out[i] = e + o
        out[i + 1] = e - o

    pair(1, jx, xx, axis_r + 2.0 * (a + c))
    pair(3, jy, yy, axis_r + 2.0 * (a + b))
    pair(5, jz, zz, axis_r + 2.0 * (b + c))
    for i, u, even in ((7, jx + jy, plane_r - a), (9, jx - jy, plane_r - a), (11, jx + jz, plane_r - c),
                       (13, jx - jz, plane_r - c), (15, jy + jz, plane_r - b), (17, jy - jz, plane_r - b)):
        pair(i, u, u * u, even)
    return out


def pull(own, source, y_row):
    row = lax.broadcasted_iota(jnp.int32, (YS, ZS), 0)
    mine = [own(i) for i in range(19)]
    out = [mine[0]]
    for i in range(1, 19):
        cx, cy, cz = VELOCITIES[i]
        v = source(i)
        if cy == 1:
            v = jnp.where(row == 0, y_row(i), pltpu.roll(v, 1, 0))
        elif cy == -1:
            v = jnp.where(row == YS - 1, y_row(i), pltpu.roll(v, YS - 1, 0))
        if cz:
            v = pltpu.roll(v, cz % ZS, 1)
        reflected = mine[OPPOSITE[i]]
        wall = jnp.where(v > 0.0, reflected, 2.0 * WALL_DENSITY * WEIGHTS[i] - reflected)
        out.append(jnp.where(jnp.abs(v) < HALF_BIG, v, wall))
    return out


def fetch(hbm, vmem, sem):
    return [
        pltpu.make_async_copy(
            hbm.at[:, pl.ds(c * CHUNK, CHUNK)], vmem.at[:, pl.ds(1 + c * CHUNK, CHUNK)], sem.at[c]
        )
        for c in range(CHUNKS)
    ]


def place_x_halo(f, xlo, xhi):
    first = lax.axis_index("slab") == 0
    last = lax.axis_index("slab") == lax.axis_size("slab") - 1
    for k in range(5):
        f[X_UP[k], 0] = jnp.where(first, BIG, xlo[k])
        f[X_DOWN[k], XS + 1] = jnp.where(last, BIG, xhi[k])


def y_rows(ylo, yhi, x):
    first = lax.axis_index("blk") == 0
    last = lax.axis_index("blk") == lax.axis_size("blk") - 1

    def y_row(i):
        at = x + 1 - VELOCITIES[i][0]
        if i in Y_UP:
            return jnp.where(first, BIG, ylo[Y_UP.index(i), pl.ds(at, 1), :])
        return jnp.where(last, BIG, yhi[Y_DOWN.index(i), pl.ds(at, 1), :])

    return y_row


def step_one_kernel(pops, solid, wetting, xlo, xhi, ylo, yhi, out, xup, xdn, yup, ydn, f, mark, res, sem_in, sem_out):
    copies = fetch(pops, f, sem_in)
    for copy in copies:
        copy.start()
    place_x_halo(f, xlo, xhi)
    mark[0] = jnp.zeros((YS, ZS), jnp.float32)
    mark[XS + 1] = jnp.zeros((YS, ZS), jnp.float32)

    def marks(x, carry):
        mark[x + 1] = jnp.where(solid[x] == 1, jnp.where(wetting[x] == 1, -BIG, BIG), 0.0)
        return carry

    lax.fori_loop(0, XS, marks, 0)

    def plane(x, carry):
        marked = {c: mark[x + 1 - c] for c in (-1, 0, 1)}

        def source(i):
            c = VELOCITIES[i][0]
            return jnp.where(marked[c] == 0.0, f[i, x + 1 - c], marked[c])

        pulled = pull(lambda i: f[i, x + 1], source, y_rows(ylo, yhi, x))
        new = collide(pulled)
        here = marked[0]
        for i in range(19):
            value = jnp.where(here == 0.0, new[i], here)
            res[i, x] = value
            if i in Y_UP:
                yup[Y_UP.index(i), pl.ds(x + 1, 1), :] = value[YS - 1 : YS]
            if i in Y_DOWN:
                ydn[Y_DOWN.index(i), pl.ds(x + 1, 1), :] = value[0:1]
        return carry

    outs = []
    copies[0].wait()
    for c in range(CHUNKS):
        if c + 1 < CHUNKS:
            copies[c + 1].wait()
        lax.fori_loop(c * CHUNK, (c + 1) * CHUNK, plane, 0)
        at = pl.ds(c * CHUNK, CHUNK)
        outs.append(pltpu.make_async_copy(res.at[:, at], out.at[:, at], sem_out.at[c]))
        outs[-1].start()
    for k in range(5):
        xup[k] = res[X_UP[k], XS - 1]
        xdn[k] = res[X_DOWN[k], 0]
    for copy in outs:
        copy.wait()


def step_two_kernel(owners, f1, xlo, xhi, ylo, yhi, outgoing, f, col, buf, sem_in, sem_out):
    copies = fetch(f1, f, sem_in)
    for copy in copies:
        copy.start()
    place_x_halo(f, xlo, xhi)
    lane_block = lax.broadcasted_iota(jnp.int32, (8, ZS), 1) // 16

    def group(c):
        def plane(k, carry):
            x = c * CHUNK + k
            new = collide(
                pull(
                    lambda i: f[i, x + 1],
                    lambda i: f[i, x + 1 - VELOCITIES[i][0]],
                    y_rows(ylo, yhi, x),
                )
            )
            fluid = jnp.abs(f[0, x + 1]) < HALF_BIG
            for i in range(19):
                col[i, k] = jnp.where(fluid, new[i], 0.0)
            return carry

        lax.fori_loop(0, CHUNK, plane, 0)
        first = (c // 4) * 8

        def channel(i, carry):
            v = [col[i, r // 2, (r % 2) * 8 : (r % 2) * 8 + 8, :] for r in range(8)]
            for w in (4, 2, 1):
                high = (lane_block & w) != 0
                for r in range(8):
                    if r & w == 0:
                        a, b = v[r], v[r | w]
                        v[r] = jnp.where(high, pltpu.roll(b, 16 * w, 1), a)
                        v[r | w] = jnp.where(high, b, pltpu.roll(a, ZS - 16 * w, 1))
            at = pl.multiple_of(i * 32 + (c % 4) * 8, 8)
            for r in range(8):
                buf[first + r, pl.ds(at, 8), :] = v[r]
            return carry

        lax.fori_loop(0, 19, channel, 0)

    outs = []
    copies[0].wait()
    for c in range(CHUNKS):
        if c + 1 < CHUNKS:
            copies[c + 1].wait()
        group(c)
        if c % 4 == 3:
            for k in range((c // 4) * 8, (c // 4) * 8 + 8):
                outs.append(pltpu.make_async_copy(buf.at[k], outgoing.at[owners[k]], sem_out.at[k]))
                outs[-1].start()
    for copy in outs:
        copy.wait()


def place_kernel(sources, incoming, out, rows):
    del sources
    sub = lax.broadcasted_iota(jnp.int32, (8, ZS), 0)
    lane_block = lax.broadcasted_iota(jnp.int32, (8, ZS), 1) // 16
    pick = (lane_block + sub + 1) & 7
    for i in range(19):
        for q in range(4):
            v = incoming[0, i * 32 + q * 8 : i * 32 + q * 8 + 8, :]
            v = pltpu.roll(v, 0, 1, stride=16, stride_axis=0)
            v = jnp.take_along_axis(v, pick, axis=0)
            v = pltpu.roll(v, 16, 1, stride=16, stride_axis=0)
            rows[pl.ds(i * PITCH + q * 8, 8), :] = v
    for j in range(32):
        out[0, :, j * 128 : (j + 1) * 128] = rows[pl.ds(j // 8 * 8 + 7 - j % 8, 19, stride=PITCH), :]


VMEM = pl.BlockSpec(memory_space=pltpu.VMEM)
ANY = pl.BlockSpec(memory_space=pl.ANY)
SMEM = pl.BlockSpec(memory_space=pltpu.SMEM)


def sds(*shape):
    return jax.ShapeDtypeStruct(shape, jnp.float32)


def params():
    return pltpu.CompilerParams(vmem_limit_bytes=48 * 1024 * 1024)


def step_one(pops, solid, wetting, halo):
    return pl.pallas_call(
        step_one_kernel,
        out_shape=(sds(19, XS, YS, ZS), sds(5, YS, ZS), sds(5, YS, ZS), sds(5, HALO_ROWS, ZS), sds(5, HALO_ROWS, ZS)),
        in_specs=[ANY] + [VMEM] * 6,
        out_specs=(ANY, VMEM, VMEM, VMEM, VMEM),
        scratch_shapes=[
            pltpu.VMEM((19, XS + 2, YS, ZS), jnp.float32),
            pltpu.VMEM((XS + 2, YS, ZS), jnp.float32),
            pltpu.VMEM((19, XS, YS, ZS), jnp.float32),
            pltpu.SemaphoreType.DMA((CHUNKS,)),
            pltpu.SemaphoreType.DMA((CHUNKS,)),
        ],
        compiler_params=params(),
        name="step_one",
    )(pops, solid, wetting, *halo)


def step_two(owners, f1, halo, peers):
    return pl.pallas_call(
        step_two_kernel,
        out_shape=sds(peers, BLOCK_ROWS, ZS),
        in_specs=[SMEM, ANY] + [VMEM] * 4,
        out_specs=ANY,
        scratch_shapes=[
            pltpu.VMEM((19, XS + 2, YS, ZS), jnp.float32),
            pltpu.VMEM((19, CHUNK, YS, ZS), jnp.float32),
            pltpu.VMEM((BLOCKS, BLOCK_ROWS, ZS), jnp.float32),
            pltpu.SemaphoreType.DMA((CHUNKS,)),
            pltpu.SemaphoreType.DMA((BLOCKS,)),
        ],
        compiler_params=params(),
        name="step_two",
    )(owners, f1, *halo)


def place(sources, incoming):
    return pl.pallas_call(
        place_kernel,
        out_shape=sds(BLOCKS, 19, 4096),
        grid_spec=pltpu.PrefetchScalarGridSpec(
            num_scalar_prefetch=1,
            grid=(BLOCKS,),
            in_specs=[pl.BlockSpec((1, BLOCK_ROWS, ZS), lambda j, src: (src[j], 0, 0))],
            out_specs=pl.BlockSpec((1, 19, 4096), lambda j, src: (j, 0, 0)),
            scratch_shapes=[pltpu.VMEM((640, ZS), jnp.float32)],
        ),
        compiler_params=params(),
        name="place",
    )(sources, incoming)


def shift(value, axis, up):
    count = lax.axis_size(axis)
    steps = [(i, i + 1) if up else (i + 1, i) for i in range(count - 1)]
    return lax.ppermute(value, axis, steps)


def exchange(xup, xdn, yup, ydn):
    xlo, xhi = shift(xup, "slab", True), shift(xdn, "slab", False)
    first = lax.axis_index("slab") == 0
    last = lax.axis_index("slab") == lax.axis_size("slab") - 1
    row = jnp.arange(HALO_ROWS)[:, None]

    def corners(rows, lo_channel, hi_channel, y, channels):
        parts = []
        for k, i in enumerate(channels):
            part = rows[k]
            if i == lo_channel:
                part = jnp.where(row == 0, jnp.where(first, BIG, xlo[X_UP.index(i), y]), part)
            if i == hi_channel:
                part = jnp.where(row == XS + 1, jnp.where(last, BIG, xhi[X_DOWN.index(i), y]), part)
            parts.append(part)
        return jnp.stack(parts)

    yup = corners(yup, 7, 10, YS - 1, Y_UP)
    ydn = corners(ydn, 9, 8, 0, Y_DOWN)
    return xlo, xhi, shift(yup, "blk", True), shift(ydn, "blk", False)


def per_device(populations, solid, wetting, dest):
    me = lax.axis_index("blk")
    peers = lax.axis_size("blk")
    everyone = lax.all_gather(dest[0], "blk")
    mark = jnp.where(solid == 1, jnp.where(wetting == 1, -BIG, BIG), 0.0)

    def marked(channels, x, y):
        m = mark[x, y]
        return jnp.where(m == 0.0, jnp.stack([populations[i, x, y] for i in channels]), m)

    every = slice(None)
    grow = ((0, 0), (1, HALO_ROWS - XS - 1), (0, 0))
    halo = exchange(
        marked(X_UP, XS - 1, every),
        marked(X_DOWN, 0, every),
        jnp.pad(marked(Y_UP, every, YS - 1), grow),
        jnp.pad(marked(Y_DOWN, every, 0), grow),
    )
    f1, *edges = step_one(populations, solid, wetting, halo)
    outgoing = step_two(dest[0] // BLOCKS, f1, exchange(*edges), peers)
    incoming = lax.all_to_all(outgoing, "blk", split_axis=0, concat_axis=0, tiled=True)
    mine = everyone // BLOCKS == me
    sources = jnp.sum(jnp.where(mine, jnp.arange(peers, dtype=jnp.int32)[:, None], 0), axis=0)
    return place(sources, incoming)


def solution(mesh):
    in_specs = (
        P(None, "slab", "blk", None),
        P("slab", "blk", None),
        P("slab", "blk", None),
        P("slab", "blk"),
    )
    out_specs = P(("slab", "blk"), None, None)
    return jax.shard_map(
        per_device, mesh=mesh, in_specs=in_specs, out_specs=out_specs, check_vma=False
    )
```

profile of v0, /device:TPU:1, one launch (start us, length us, event | category | flops | bytes accessed | tf_op | source)
XLA Modules:
  0.0 289.6 jit_solution(14909662921952405863)
XLA Ops:
  0.0 1.1 select_select_fusion
  1.1 0.7 constant_dynamic-update-slice_fusion.9
  1.8 0.7 constant_dynamic-update-slice_fusion.8
  2.6 0.7 constant_dynamic-update-slice_fusion.7
  3.3 0.7 constant_dynamic-update-slice_fusion.6
  4.0 0.7 constant_dynamic-update-slice_fusion.5
  4.7 1.3 collective-permute-start.1
  6.0 4.6 %collective-permute-start = (f32[5,16,128]{2,1,0:T(8,128)S(1)}, f32[5,16,128]{2,1,0:T(8,128)S(1)}, u32[]{:S(2)}, u32[]{:S(2)}) collective-permute-start(f32[5,16,128]{2,1,0:T(8,128)S(1)} %broadcast_select_fusion.3), channel_id=1, source_target_pairs={{0,32},{32,64},{64,96},{1,33},{33,65},{65,97},{2,34},{34,66},{66,9... | collective-permute-start | bytes 122888 | tf_op jit(solution)/shard_map/ppermute | solution.py:315
  10.6 1.5 fusion.15
  12.4 0.0 collective-permute-done.1.xhi
  12.4 0.0 collective-permute-done.xlo
  12.4 0.1 pad_slice_fusion.3
  12.5 4.9 %collective-permute-start.2 = (f32[5,40,128]{2,1,0:T(8,128)S(1)}, f32[5,40,128]{2,1,0:T(8,128)S(1)}, u32[]{:S(2)}, u32[]{:S(2)}) collective-permute-start(f32[5,40,128]{2,1,0:T(8,128)S(1)} %pad_maximum_fusion), channel_id=1, source_target_pairs={{0,1},{1,2},{2,3},{3,4},{4,5},{5,6},{6,7},{7,8},{8,9},{9,10},{10,1... | collective-permute-start | bytes 307208 | tf_op jit(solution)/shard_map/ppermute | solution.py:315
  17.5 1.9 collective-permute-start.3
  19.4 4.0 %collective-permute-done.3.yhi = f32[5,40,128]{2,1,0:T(8,128)S(1)} collective-permute-done((f32[5,40,128]{2,1,0:T(8,128)S(1)}, f32[5,40,128]{2,1,0:T(8,128)S(1)}, u32[]{:S(2)}, u32[]{:S(2)}) %collective-permute-start.3) | collective-permute-done | bytes 102432 | tf_op jit(solution)/shard_map/ppermute | solution.py:315
  23.4 0.9 copy-done
  24.4 0.9 copy-done.1
  25.3 6.8 %step_one.1 = (f32[19,32,16,128]{3,2,1,0:T(8,128)S(1)}, f32[5,16,128]{2,1,0:T(8,128)S(1)}, f32[5,16,128]{2,1,0:T(8,128)S(1)}, f32[5,40,128]{2,1,0:T(8,128)S(1)}, f32[5,40,128]{2,1,0:T(8,128)S(1)}) custom-call(f32[19,32,16,128]{3,2,1,0:T(8,128)} %pops.1, s32[32,16,128]{2,1,0:T(8,128)S(1)} %copy-done, s32[32,16,128]{2,1,0:T(8,128)S(1)} %copy-done.1, ...), custom_call_target="tpu_custom_call" | custom-call | tf_op jit(solution)/shard_map/step_one/pallas_call | solution.py:261
  32.1 3.8 %collective-permute-start.4 = (f32[5,16,128]{2,1,0:T(8,128)S(1)}, f32[5,16,128]{2,1,0:T(8,128)S(1)}, u32[]{:S(2)}, u32[]{:S(2)}) collective-permute-start(f32[5,16,128]{2,1,0:T(8,128)S(1)} %get-tuple-element.11), channel_id=1, source_target_pairs={{0,32},{32,64},{64,96},{1,33},{33,65},{65,97},{2,34},{34,66},{66,9... | collective-permute-start | bytes 122888 | tf_op jit(solution)/shard_map/ppermute | solution.py:315
  36.0 1.3 collective-permute-start.5
  37.3 3.4 %collective-permute-done.5.xhi = f32[5,16,128]{2,1,0:T(8,128)S(1)} collective-permute-done((f32[5,16,128]{2,1,0:T(8,128)S(1)}, f32[5,16,128]{2,1,0:T(8,128)S(1)}, u32[]{:S(2)}, u32[]{:S(2)}) %collective-permute-start.5) | collective-permute-done | bytes 40992 | tf_op jit(solution)/shard_map/ppermute | solution.py:315
  40.7 0.1 fusion.18
  40.8 3.2 %collective-permute-start.6 = (f32[5,40,128]{2,1,0:T(8,128)S(1)}, f32[5,40,128]{2,1,0:T(8,128)S(1)}, u32[]{:S(2)}, u32[]{:S(2)}) collective-permute-start(f32[5,40,128]{2,1,0:T(8,128)S(1)} %pad_maximum_fusion.2), channel_id=1, source_target_pairs={{0,1},{1,2},{2,3},{3,4},{4,5},{5,6},{6,7},{7,8},{8,9},{9,10},{10,1... | collective-permute-start | bytes 307208 | tf_op jit(solution)/shard_map/ppermute | solution.py:315
  44.1 0.1 fusion.17
  44.2 1.9 collective-permute-start.7
  46.1 0.0 collective-permute-done.6.ylo
  46.2 4.0 %collective-permute-done.7.yhi = f32[5,40,128]{2,1,0:T(8,128)S(1)} collective-permute-done((f32[5,40,128]{2,1,0:T(8,128)S(1)}, f32[5,40,128]{2,1,0:T(8,128)S(1)}, u32[]{:S(2)}, u32[]{:S(2)}) %collective-permute-start.7) | collective-permute-done | bytes 102432 | tf_op jit(solution)/shard_map/ppermute | solution.py:315
  50.2 40.5 %step_two.1 = f32[32,608,128]{2,1,0:T(8,128)} custom-call(s32[16]{0:T(128)S(1)} %and_select_fusion.owners, f32[19,32,16,128]{3,2,1,0:T(8,128)S(1)} %get-tuple-element.10.f1, f32[5,16,128]{2,1,0:T(8,128)S(1)} %collective-permute-done.4.xlo, f32[5,16,128]{2,1,0:T(8,128)S(1)} %collective-permute-done.5.xhi, f32[5,40,128]{2,1,0:T(8,128)S(1)} %collective-permute-done.6.ylo, ...), custom_call_target="tpu_custom_call" | custom-call | tf_op jit(solution)/shard_map/step_two/pallas_call | solution.py:279
  90.7 10.5 %all-to-all-start = ((f32[32,608,128]{2,1,0:T(8,128)}), f32[32,608,128]{2,1,0:T(8,128)}, u32[]{:S(2)}, u32[]{:S(2)}) async-start(f32[32,608,128]{2,1,0:T(8,128)} %step_two.1), calls=%async_computation | async-start | bytes 19922944 | tf_op jit(solution)/shard_map/all_to_all | solution.py:360
  101.2 166.7 %all-gather = s32[32,1,16]{2,1,0:T(1,128)S(1)} all-gather(s32[1,1,16]{2,1,0:T(1,128)S(1)} %bitcast.103), channel_id=1, replica_groups=mesh['slab'=4,'blk'=32] {'blk'}, dimensions={0}, use_global_device_ids=true | all-gather | bytes 2112 | tf_op jit(solution)/shard_map/all_gather | solution.py:343
  268.0 13.6 %place.1 = f32[16,19,4096]{2,1,0:T(8,128)} custom-call(s32[16]{0:T(128)S(1)} %select_reduce_fusion.sources, f32[32,608,128]{2,1,0:T(8,128)} %all-to-all-done.incoming), custom_call_target="tpu_custom_call" | custom-call | tf_op jit(solution)/shard_map/place/pallas_call | solution.py:297
  281.6 7.9 %copy.28 = f32[16,19,4096]{2,0,1:T(8,128)} copy(f32[16,19,4096]{2,1,0:T(8,128)} %place.1) | data formatting | bytes 9961472 | tf_op jit(solution)/shard_map/place/pallas_call | solution.py:297
  (42 shorter events, 0.3 us)
Async XLA Ops:
  0.0 46.1 %copy-start.2 = (s32[1,16]{1,0:T(1,128)S(1)}, s32[1,16]{1,0:T(1,128)}, u32[]{:S(2)}) copy-start(s32[1,16]{1,0:T(1,128)} %param.7) | copy-start | bytes 196
  4.7 7.7 %collective-permute-start.1 = (f32[5,16,128]{2,1,0:T(8,128)S(1)}, f32[5,16,128]{2,1,0:T(8,128)S(1)}, u32[]{:S(2)}, u32[]{:S(2)}) collective-permute-start(f32[5,16,128]{2,1,0:T(8,128)S(1)} %broadcast_select_fusion.2), channel_id=1, source_target_pairs={{32,0},{64,32},{96,64},{33,1},{65,33},{97,65},{34,2},{66,34},{98,6... | collective-permute-start | bytes 122888 | tf_op jit(solution)/shard_map/ppermute | solution.py:315
  6.0 6.4 %collective-permute-start = (f32[5,16,128]{2,1,0:T(8,128)S(1)}, f32[5,16,128]{2,1,0:T(8,128)S(1)}, u32[]{:S(2)}, u32[]{:S(2)}) collective-permute-start(f32[5,16,128]{2,1,0:T(8,128)S(1)} %broadcast_select_fusion.3), channel_id=1, source_target_pairs={{0,32},{32,64},{64,96},{1,33},{33,65},{65,97},{2,34},{34,66},{66,9... | collective-permute-start | bytes 122888 | tf_op jit(solution)/shard_map/ppermute | solution.py:315
  12.5 6.9 %collective-permute-start.2 = (f32[5,40,128]{2,1,0:T(8,128)S(1)}, f32[5,40,128]{2,1,0:T(8,128)S(1)}, u32[]{:S(2)}, u32[]{:S(2)}) collective-permute-start(f32[5,40,128]{2,1,0:T(8,128)S(1)} %pad_maximum_fusion), channel_id=1, source_target_pairs={{0,1},{1,2},{2,3},{3,4},{4,5},{5,6},{6,7},{7,8},{8,9},{9,10},{10,1... | collective-permute-start | bytes 307208 | tf_op jit(solution)/shard_map/ppermute | solution.py:315
  17.5 6.0 %collective-permute-start.3 = (f32[5,40,128]{2,1,0:T(8,128)S(1)}, f32[5,40,128]{2,1,0:T(8,128)S(1)}, u32[]{:S(2)}, u32[]{:S(2)}) collective-permute-start(f32[5,40,128]{2,1,0:T(8,128)S(1)} %pad_maximum_fusion.1), channel_id=1, source_target_pairs={{1,0},{2,1},{3,2},{4,3},{5,4},{6,5},{7,6},{8,7},{9,8},{10,9},{11,1... | collective-permute-start | bytes 307208 | tf_op jit(solution)/shard_map/ppermute | solution.py:315
  23.4 1.0 copy-start
  24.4 0.9 copy-start.1
  32.1 5.1 %collective-permute-start.4 = (f32[5,16,128]{2,1,0:T(8,128)S(1)}, f32[5,16,128]{2,1,0:T(8,128)S(1)}, u32[]{:S(2)}, u32[]{:S(2)}) collective-permute-start(f32[5,16,128]{2,1,0:T(8,128)S(1)} %get-tuple-element.11), channel_id=1, source_target_pairs={{0,32},{32,64},{64,96},{1,33},{33,65},{65,97},{2,34},{34,66},{66,9... | collective-permute-start | bytes 122888 | tf_op jit(solution)/shard_map/ppermute | solution.py:315
  36.0 4.7 %collective-permute-start.5 = (f32[5,16,128]{2,1,0:T(8,128)S(1)}, f32[5,16,128]{2,1,0:T(8,128)S(1)}, u32[]{:S(2)}, u32[]{:S(2)}) collective-permute-start(f32[5,16,128]{2,1,0:T(8,128)S(1)} %get-tuple-element.12), channel_id=1, source_target_pairs={{32,0},{64,32},{96,64},{33,1},{65,33},{97,65},{34,2},{66,34},{98,6... | collective-permute-start | bytes 122888 | tf_op jit(solution)/shard_map/ppermute | solution.py:315
  40.8 5.3 %collective-permute-start.6 = (f32[5,40,128]{2,1,0:T(8,128)S(1)}, f32[5,40,128]{2,1,0:T(8,128)S(1)}, u32[]{:S(2)}, u32[]{:S(2)}) collective-permute-start(f32[5,40,128]{2,1,0:T(8,128)S(1)} %pad_maximum_fusion.2), channel_id=1, source_target_pairs={{0,1},{1,2},{2,3},{3,4},{4,5},{5,6},{6,7},{7,8},{8,9},{9,10},{10,1... | collective-permute-start | bytes 307208 | tf_op jit(solution)/shard_map/ppermute | solution.py:315
  44.2 6.0 %collective-permute-start.7 = (f32[5,40,128]{2,1,0:T(8,128)S(1)}, f32[5,40,128]{2,1,0:T(8,128)S(1)}, u32[]{:S(2)}, u32[]{:S(2)}) collective-permute-start(f32[5,40,128]{2,1,0:T(8,128)S(1)} %pad_maximum_fusion.3), channel_id=1, source_target_pairs={{1,0},{2,1},{3,2},{4,3},{5,4},{6,5},{7,6},{8,7},{9,8},{10,9},{11,1... | collective-permute-start | bytes 307208 | tf_op jit(solution)/shard_map/ppermute | solution.py:315
  90.7 177.3 %all-to-all-start = ((f32[32,608,128]{2,1,0:T(8,128)}), f32[32,608,128]{2,1,0:T(8,128)}, u32[]{:S(2)}, u32[]{:S(2)}) async-start(f32[32,608,128]{2,1,0:T(8,128)} %step_two.1), calls=%async_computation | async-start | bytes 19922944 | tf_op jit(solution)/shard_map/all_to_all | solution.py:360
where the time goes:
time: 292 us; the launch traced here: 290 us
  blocking collectives  167 us (57%)
  Pallas kernels  60.9 us (21%)
  starting transfers between devices  33.5 us (11%)
  local copies, waits for them, and re-layouts  15 us (5%)
  waiting for transfers between devices  11.5 us (4%)
    all_gather x1, blocking collectives, per_device(): everyone = lax.all_gather(dest[0], 'blk')  167 us
    pallas_call x1, Pallas kernels, step_two(): pl.pallas_call(step_two_kernel, out_shape=sds(peers, BLOCK_ROWS, ZS), in_...  40.5 us
    ppermute x8, starting transfers between devices, shift(): return lax.ppermute(value, axis, steps)  23 us
    pallas_call x1, Pallas kernels, place(): pl.pallas_call(place_kernel, out_shape=sds(BLOCKS, 19, 4096), grid_spec=p...  13.6 us
    ppermute x8, waiting for transfers between devices, shift(): return lax.ppermute(value, axis, steps)  11.5 us
    all_to_all x1, starting transfers between devices, per_device(): lax.all_to_all(outgoing, 'blk', split_axis=0, concat_axis=0, tiled=True)  10.5 us
    pallas_call x1, local copies, waits for them, and re-layouts, place(): pl.pallas_call(place_kernel, out_shape=sds(BLOCKS, 19, 4096), grid_spec=p...  7.94 us
    pallas_call x1, Pallas kernels, step_one(): pl.pallas_call(step_one_kernel, out_shape=(sds(19, XS, YS, ZS), sds(5, YS...  6.79 us
  transfers between devices with their start and end apart: 9, of which 3 were waited for; matrix products, arithmetic and copies ran while one was open for 1% of the time, Pallas kernels for 0%

commit v1 on v0

--- a/solution.py
+++ b/solution.py
@@ -30,7 +30,7 @@
 CHUNKS = XS // CHUNK
 BLOCKS = 16
 BLOCK_ROWS = 19 * 32
-PITCH = 33
+SLOT_ROWS = BLOCK_ROWS + 8
 
 
 def collide(f):
@@ -173,75 +173,106 @@
         copy.wait()
 
 
-def step_two_kernel(owners, f1, xlo, xhi, ylo, yhi, outgoing, f, col, buf, sem_in, sem_out):
+def step_two_kernel(owners, f1, xlo, xhi, ylo, yhi, outgoing, f, buf, absent, sem_in, sem_absent, sem_out):
     copies = fetch(f1, f, sem_in)
     for copy in copies:
         copy.start()
+    absent[...] = jnp.full((8, ZS), -1.0, jnp.float32)
+    label_rows = pl.ds(BLOCK_ROWS, 8)
+    clears = [
+        pltpu.make_async_copy(absent, outgoing.at[p, label_rows], sem_absent.at[p])
+        for p in range(outgoing.shape[0])
+    ]
+    for clear in clears:
+        clear.start()
+    for k in range(BLOCKS):
+        at = (k // 8 * 8 + 7 - k % 8) * SLOT_ROWS + BLOCK_ROWS
+        buf[at : at + 8, :] = jnp.full((8, ZS), float(k), jnp.float32)
     place_x_halo(f, xlo, xhi)
+    sub = lax.broadcasted_iota(jnp.int32, (8, ZS), 0)
     lane_block = lax.broadcasted_iota(jnp.int32, (8, ZS), 1) // 16
-
-    def group(c):
-        def plane(k, carry):
-            x = c * CHUNK + k
-            new = collide(
-                pull(
-                    lambda i: f[i, x + 1],
-                    lambda i: f[i, x + 1 - VELOCITIES[i][0]],
-                    y_rows(ylo, yhi, x),
-                )
+    pick = (lane_block + sub + 1) & 7
+
+    def plane(x, carry):
+        new = collide(
+            pull(
+                lambda i: f[i, x + 1],
+                lambda i: f[i, x + 1 - VELOCITIES[i][0]],
+                y_rows(ylo, yhi, x),
             )
-            fluid = jnp.abs(f[0, x + 1]) < HALF_BIG
-            for i in range(19):
-                col[i, k] = jnp.where(fluid, new[i], 0.0)
-            return carry
-
-        lax.fori_loop(0, CHUNK, plane, 0)
-        first = (c // 4) * 8
-
-        def channel(i, carry):
-            v = [col[i, r // 2, (r % 2) * 8 : (r % 2) * 8 + 8, :] for r in range(8)]
-            for w in (4, 2, 1):
-                high = (lane_block & w) != 0
-                for r in range(8):
-                    if r & w == 0:
-                        a, b = v[r], v[r | w]
-                        v[r] = jnp.where(high, pltpu.roll(b, 16 * w, 1), a)
-                        v[r | w] = jnp.where(high, b, pltpu.roll(a, ZS - 16 * w, 1))
-            at = pl.multiple_of(i * 32 + (c % 4) * 8, 8)
-            for r in range(8):
-                buf[first + r, pl.ds(at, 8), :] = v[r]
-            return carry
-
-        lax.fori_loop(0, 19, channel, 0)
+        )
+        fluid = jnp.abs(f[0, x + 1]) < HALF_BIG
+        base = x // 16 * (8 * SLOT_ROWS) + x % 16 * 2
+        for i in range(19):
+            value = jnp.where(fluid, new[i], 0.0)
+            for half in range(2):
+                v = pltpu.roll(value[half * 8 : half * 8 + 8], 0, 1, stride=16, stride_axis=0)
+                v = jnp.take_along_axis(v, pick, axis=0)
+                v = pltpu.roll(v, 16, 1, stride=16, stride_axis=0)
+                buf[pl.ds(base + i * 32 + half, 8, stride=SLOT_ROWS + 1), :] = v
+        return carry
 
     outs = []
     copies[0].wait()
     for c in range(CHUNKS):
         if c + 1 < CHUNKS:
             copies[c + 1].wait()
-        group(c)
+        lax.fori_loop(c * CHUNK, (c + 1) * CHUNK, plane, 0)
+        if c == 0:
+            for clear in clears:
+                clear.wait()
         if c % 4 == 3:
-            for k in range((c // 4) * 8, (c // 4) * 8 + 8):
-                outs.append(pltpu.make_async_copy(buf.at[k], outgoing.at[owners[k]], sem_out.at[k]))
+            for k in range(c // 4 * 8, c // 4 * 8 + 8):
+                at = (k // 8 * 8 + 7 - k % 8) * SLOT_ROWS
+                outs.append(
+                    pltpu.make_async_copy(
+                        buf.at[pl.ds(at, SLOT_ROWS)], outgoing.at[owners[k]], sem_out.at[k]
+                    )
+                )
                 outs[-1].start()
     for copy in outs:
         copy.wait()
 
 
-def place_kernel(sources, incoming, out, rows):
-    del sources
-    sub = lax.broadcasted_iota(jnp.int32, (8, ZS), 0)
-    lane_block = lax.broadcasted_iota(jnp.int32, (8, ZS), 1) // 16
-    pick = (lane_block + sub + 1) & 7
-    for i in range(19):
-        for q in range(4):
-            v = incoming[0, i * 32 + q * 8 : i * 32 + q * 8 + 8, :]
-            v = pltpu.roll(v, 0, 1, stride=16, stride_axis=0)
-            v = jnp.take_along_axis(v, pick, axis=0)
-            v = pltpu.roll(v, 16, 1, stride=16, stride_axis=0)
-            rows[pl.ds(i * PITCH + q * 8, 8), :] = v
-    for j in range(32):
-        out[0, :, j * 128 : (j + 1) * 128] = rows[pl.ds(j // 8 * 8 + 7 - j % 8, 19, stride=PITCH), :]
+def place_kernel(incoming, out, labels, blocks, res, sem_label, sem_in, sem_out):
+    peers = incoming.shape[0]
+    copy = pltpu.make_async_copy(incoming.at[:, pl.ds(BLOCK_ROWS, 8)], labels, sem_label)
+    copy.start()
+    copy.wait()
+    lane = lax.broadcasted_iota(jnp.int32, (1, ZS), 1)
+    slot = lane.astype(jnp.float32)
+    found = jnp.zeros((1, ZS), jnp.int32)
+    for p in range(peers):
+        found += jnp.where(labels[p, 7:8, :] == slot, p, 0)
+    ins = []
+    for k in range(BLOCKS):
+        source = jnp.clip(jnp.sum(jnp.where(lane == k, found, 0)), 0, peers - 1)
+        ins.append(
+            pltpu.make_async_copy(
+                incoming.at[source], blocks.at[pl.ds(k * SLOT_ROWS, SLOT_ROWS)], sem_in.at[k]
+            )
+        )
+        ins[-1].start()
+    outs = []
+    for h in range(2):
+        for k in range(8):
+            ins[h * 8 + k].wait()
+
+        def channel(i, carry):
+            for j in range(32):
+                at = h * 8 * SLOT_ROWS + 7 + i * 32 + j
+                res[i, h * 8 : h * 8 + 8, j * 128 : (j + 1) * 128] = blocks[
+                    pl.ds(at, 8, stride=SLOT_ROWS - 1), :
+                ]
+            return carry
+
+        for part, (low, high) in enumerate(((0, 5), (5, 10), (10, 15), (15, 19))):
+            lax.fori_loop(low, high, channel, 0)
+            at = (pl.ds(low, high - low), pl.ds(h * 8, 8))
+            outs.append(pltpu.make_async_copy(res.at[at], out.at[at], sem_out.at[h * 4 + part]))
+            outs[-1].start()
+    for copy in outs:
+        copy.wait()
 
 
 VMEM = pl.BlockSpec(memory_space=pltpu.VMEM)
@@ -278,14 +309,15 @@
 def step_two(owners, f1, halo, peers):
     return pl.pallas_call(
         step_two_kernel,
-        out_shape=sds(peers, BLOCK_ROWS, ZS),
+        out_shape=sds(peers, SLOT_ROWS, ZS),
         in_specs=[SMEM, ANY] + [VMEM] * 4,
         out_specs=ANY,
         scratch_shapes=[
             pltpu.VMEM((19, XS + 2, YS, ZS), jnp.float32),
-            pltpu.VMEM((19, CHUNK, YS, ZS), jnp.float32),
-            pltpu.VMEM((BLOCKS, BLOCK_ROWS, ZS), jnp.float32),
+            pltpu.VMEM((BLOCKS * SLOT_ROWS, ZS), jnp.float32),
+            pltpu.VMEM((8, ZS), jnp.float32),
             pltpu.SemaphoreType.DMA((CHUNKS,)),
+            pltpu.SemaphoreType.DMA((peers,)),
             pltpu.SemaphoreType.DMA((BLOCKS,)),
         ],
         compiler_params=params(),
@@ -293,20 +325,24 @@
     )(owners, f1, *halo)
 
 
-def place(sources, incoming):
+def place(incoming):
+    peers = incoming.shape[0]
     return pl.pallas_call(
         place_kernel,
-        out_shape=sds(BLOCKS, 19, 4096),
-        grid_spec=pltpu.PrefetchScalarGridSpec(
-            num_scalar_prefetch=1,
-            grid=(BLOCKS,),
-            in_specs=[pl.BlockSpec((1, BLOCK_ROWS, ZS), lambda j, src: (src[j], 0, 0))],
-            out_specs=pl.BlockSpec((1, 19, 4096), lambda j, src: (j, 0, 0)),
-            scratch_shapes=[pltpu.VMEM((640, ZS), jnp.float32)],
-        ),
+        out_shape=sds(19, BLOCKS, 4096),
+        in_specs=[ANY],
+        out_specs=ANY,
+        scratch_shapes=[
+            pltpu.VMEM((peers, 8, ZS), jnp.float32),
+            pltpu.VMEM((BLOCKS * SLOT_ROWS, ZS), jnp.float32),
+            pltpu.VMEM((19, BLOCKS, 4096), jnp.float32),
+            pltpu.SemaphoreType.DMA,
+            pltpu.SemaphoreType.DMA((BLOCKS,)),
+            pltpu.SemaphoreType.DMA((8,)),
+        ],
         compiler_params=params(),
         name="place",
-    )(sources, incoming)
+    )(incoming)
 
 
 def shift(value, axis, up):
@@ -338,9 +374,7 @@
 
 
 def per_device(populations, solid, wetting, dest):
-    me = lax.axis_index("blk")
     peers = lax.axis_size("blk")
-    everyone = lax.all_gather(dest[0], "blk")
     mark = jnp.where(solid == 1, jnp.where(wetting == 1, -BIG, BIG), 0.0)
 
     def marked(channels, x, y):
@@ -358,9 +392,7 @@
     f1, *edges = step_one(populations, solid, wetting, halo)
     outgoing = step_two(dest[0] // BLOCKS, f1, exchange(*edges), peers)
     incoming = lax.all_to_all(outgoing, "blk", split_axis=0, concat_axis=0, tiled=True)
-    mine = everyone // BLOCKS == me
-    sources = jnp.sum(jnp.where(mine, jnp.arange(peers, dtype=jnp.int32)[:, None], 0), axis=0)
-    return place(sources, incoming)
+    return place(incoming).transpose(1, 0, 2)
 
 
 def solution(mesh):

time: 292 us -> 194 us (0.66)
  blocking collectives: 167 us -> 125 us
  Pallas kernels: 60.9 us -> 24.7 us
  starting transfers between devices: 33.5 us -> 23 us
  local copies, waits for them, and re-layouts: 15 us -> 7.06 us
    all_gather x1 -> x0, blocking collectives: 167 us -> none  [per_device(): everyone = lax.all_gather(dest[0], 'blk')]
    all_to_all x0 -> x1, blocking collectives: none -> 125 us  [per_device(): lax.all_to_all(outgoing, 'blk', split_axis=0, concat_axis=0, tiled=True)]
    pallas_call x2, Pallas kernels: 54.1 us -> 17.9 us  [the longest x1 12.6 us: step_two(): pl.pallas_call(step_two_kernel, out_shape=sds(peers, SLOT_ROWS, ZS), in_s...]
    all_to_all x1 -> x0, starting transfers between devices: 10.5 us -> none  [per_device(): lax.all_to_all(outgoing, 'blk', split_axis=0, concat_axis=0, tiled=True)]
    pallas_call x1 -> x0, local copies, waits for them, and re-layouts: 7.94 us -> none  [place(): pl.pallas_call(place_kernel, out_shape=sds(BLOCKS, 19, 4096), grid_spec=p...]
  transfers between devices with their start and end apart: 9 -> 8, of which waited for: 3 -> 3; matrix products, arithmetic and copies ran while one was open for 1% -> 1% of each run, Pallas kernels for 0% -> 0%
where the time goes in v1:
time: 194 us; the launch traced here: 193 us
  blocking collectives  125 us (64%)
  Pallas kernels  24.7 us (13%)
  starting transfers between devices  23 us (12%)
  waiting for transfers between devices  11.5 us (6%)
  local copies, waits for them, and re-layouts  7.06 us (4%)
    all_to_all x1, blocking collectives, per_device(): lax.all_to_all(outgoing, 'blk', split_axis=0, concat_axis=0, tiled=True)  125 us
    ppermute x8, starting transfers between devices, shift(): return lax.ppermute(value, axis, steps)  23 us
    pallas_call x1, Pallas kernels, step_two(): pl.pallas_call(step_two_kernel, out_shape=sds(peers, SLOT_ROWS, ZS), in_s...  12.6 us
    ppermute x8, waiting for transfers between devices, shift(): return lax.ppermute(value, axis, steps)  11.5 us
    pallas_call x1, Pallas kernels, step_one(): pl.pallas_call(step_one_kernel, out_shape=(sds(19, XS, YS, ZS), sds(5, YS...  6.81 us
    pallas_call x1, Pallas kernels, place(): pl.pallas_call(place_kernel, out_shape=sds(19, BLOCKS, 4096), in_specs=[A...  5.23 us
    unnamed x18, local copies, waits for them, and re-layouts  4.8 us
  transfers between devices with their start and end apart: 8, of which 3 were waited for; matrix products, arithmetic and copies ran while one was open for 1% of the time, Pallas kernels for 0%

profile of v1, /device:TPU:1, one launch (start us, length us, event | category | flops | bytes accessed | tf_op | source)
XLA Modules:
  0.0 192.6 jit_solution(11878467285342702131)
XLA Ops:
  0.0 1.1 select_select_fusion
  1.1 0.7 constant_dynamic-update-slice_fusion.9
  1.8 0.7 constant_dynamic-update-slice_fusion.8
  2.6 0.7 constant_dynamic-update-slice_fusion.7
  3.3 0.7 constant_dynamic-update-slice_fusion.6
  4.0 0.7 constant_dynamic-update-slice_fusion.5
  4.7 1.3 collective-permute-start.1
  6.0 4.6 %collective-permute-start = (f32[5,16,128]{2,1,0:T(8,128)S(1)}, f32[5,16,128]{2,1,0:T(8,128)S(1)}, u32[]{:S(2)}, u32[]{:S(2)}) collective-permute-start(f32[5,16,128]{2,1,0:T(8,128)S(1)} %broadcast_select_fusion.3), channel_id=1, source_target_pairs={{0,32},{32,64},{64,96},{1,33},{33,65},{65,97},{2,34},{34,66},{66,9... | collective-permute-start | bytes 122888 | tf_op jit(solution)/shard_map/ppermute | solution.py:351
  10.6 1.5 fusion.12
  12.4 0.0 collective-permute-done.1.xhi
  12.4 0.0 collective-permute-done.xlo
  12.4 0.1 pad_slice_fusion.3
  12.5 4.9 %collective-permute-start.2 = (f32[5,40,128]{2,1,0:T(8,128)S(1)}, f32[5,40,128]{2,1,0:T(8,128)S(1)}, u32[]{:S(2)}, u32[]{:S(2)}) collective-permute-start(f32[5,40,128]{2,1,0:T(8,128)S(1)} %pad_maximum_fusion), channel_id=1, source_target_pairs={{0,1},{1,2},{2,3},{3,4},{4,5},{5,6},{6,7},{7,8},{8,9},{9,10},{10,1... | collective-permute-start | bytes 307208 | tf_op jit(solution)/shard_map/ppermute | solution.py:351
  17.5 1.9 collective-permute-start.3
  19.4 0.0 collective-permute-done.2.ylo
  19.4 4.0 %collective-permute-done.3.yhi = f32[5,40,128]{2,1,0:T(8,128)S(1)} collective-permute-done((f32[5,40,128]{2,1,0:T(8,128)S(1)}, f32[5,40,128]{2,1,0:T(8,128)S(1)}, u32[]{:S(2)}, u32[]{:S(2)}) %collective-permute-start.3) | collective-permute-done | bytes 102432 | tf_op jit(solution)/shard_map/ppermute | solution.py:351
  23.4 0.9 copy-done
  24.4 0.9 copy-done.1
  25.3 6.8 %step_one.1 = (f32[19,32,16,128]{3,2,1,0:T(8,128)S(1)}, f32[5,16,128]{2,1,0:T(8,128)S(1)}, f32[5,16,128]{2,1,0:T(8,128)S(1)}, f32[5,40,128]{2,1,0:T(8,128)S(1)}, f32[5,40,128]{2,1,0:T(8,128)S(1)}) custom-call(f32[19,32,16,128]{3,2,1,0:T(8,128)} %pops.1, s32[32,16,128]{2,1,0:T(8,128)S(1)} %copy-done, s32[32,16,128]{2,1,0:T(8,128)S(1)} %copy-done.1, ...), custom_call_target="tpu_custom_call" | custom-call | tf_op jit(solution)/shard_map/step_one/pallas_call | solution.py:292
  32.2 3.8 %collective-permute-start.4 = (f32[5,16,128]{2,1,0:T(8,128)S(1)}, f32[5,16,128]{2,1,0:T(8,128)S(1)}, u32[]{:S(2)}, u32[]{:S(2)}) collective-permute-start(f32[5,16,128]{2,1,0:T(8,128)S(1)} %get-tuple-element.11), channel_id=1, source_target_pairs={{0,32},{32,64},{64,96},{1,33},{33,65},{65,97},{2,34},{34,66},{66,9... | collective-permute-start | bytes 122888 | tf_op jit(solution)/shard_map/ppermute | solution.py:351
  36.0 1.3 collective-permute-start.5
  37.3 0.0 collective-permute-done.4.xlo
  37.3 3.4 %collective-permute-done.5.xhi = f32[5,16,128]{2,1,0:T(8,128)S(1)} collective-permute-done((f32[5,16,128]{2,1,0:T(8,128)S(1)}, f32[5,16,128]{2,1,0:T(8,128)S(1)}, u32[]{:S(2)}, u32[]{:S(2)}) %collective-permute-start.5) | collective-permute-done | bytes 40992 | tf_op jit(solution)/shard_map/ppermute | solution.py:351
  40.7 0.1 fusion.15
  40.8 3.2 %collective-permute-start.6 = (f32[5,40,128]{2,1,0:T(8,128)S(1)}, f32[5,40,128]{2,1,0:T(8,128)S(1)}, u32[]{:S(2)}, u32[]{:S(2)}) collective-permute-start(f32[5,40,128]{2,1,0:T(8,128)S(1)} %pad_maximum_fusion.2), channel_id=1, source_target_pairs={{0,1},{1,2},{2,3},{3,4},{4,5},{5,6},{6,7},{7,8},{8,9},{9,10},{10,1... | collective-permute-start | bytes 307208 | tf_op jit(solution)/shard_map/ppermute | solution.py:351
  44.1 0.1 fusion.14
  44.2 1.9 collective-permute-start.7
  46.2 0.0 collective-permute-done.6.ylo
  46.2 4.0 %collective-permute-done.7.yhi = f32[5,40,128]{2,1,0:T(8,128)S(1)} collective-permute-done((f32[5,40,128]{2,1,0:T(8,128)S(1)}, f32[5,40,128]{2,1,0:T(8,128)S(1)}, u32[]{:S(2)}, u32[]{:S(2)}) %collective-permute-start.7) | collective-permute-done | bytes 102432 | tf_op jit(solution)/shard_map/ppermute | solution.py:351
  50.2 12.6 %step_two.1 = f32[32,616,128]{2,1,0:T(8,128)} custom-call(s32[16]{0:T(128)S(1)} %and_select_fusion.owners, f32[19,32,16,128]{3,2,1,0:T(8,128)S(1)} %get-tuple-element.10.f1, f32[5,16,128]{2,1,0:T(8,128)S(1)} %collective-permute-done.4.xlo, f32[5,16,128]{2,1,0:T(8,128)S(1)} %collective-permute-done.5.xhi, f32[5,40,128]{2,1,0:T(8,128)S(1)} %collective-permute-done.6.ylo, ...), custom_call_target="tpu_custom_call" | custom-call | tf_op jit(solution)/shard_map/step_two/pallas_call | solution.py:310
  62.8 124.5 %all_to_all.5.incoming = f32[32,616,128]{2,1,0:T(8,128)} all-to-all(f32[32,616,128]{2,1,0:T(8,128)} %step_two.1), channel_id=1, replica_groups=mesh['slab'=4,'blk'=32] {'blk'}, dimensions={0} | all-to-all | bytes 20185088 | tf_op jit(solution)/shard_map/all_to_all | solution.py:394
  187.4 5.2 %place.1 = f32[19,16,4096]{2,1,0:T(8,128)} custom-call(f32[32,616,128]{2,1,0:T(8,128)} %all_to_all.5.incoming), custom_call_target="tpu_custom_call" | custom-call | tf_op jit(solution)/shard_map/place/pallas_call | solution.py:330
  (38 shorter events, 0.2 us)
Async XLA Ops:
  0.0 46.1 %copy-start.2 = (s32[1,16]{1,0:T(1,128)S(1)}, s32[1,16]{1,0:T(1,128)}, u32[]{:S(2)}) copy-start(s32[1,16]{1,0:T(1,128)} %param.7) | copy-start | bytes 196
  4.7 7.7 %collective-permute-start.1 = (f32[5,16,128]{2,1,0:T(8,128)S(1)}, f32[5,16,128]{2,1,0:T(8,128)S(1)}, u32[]{:S(2)}, u32[]{:S(2)}) collective-permute-start(f32[5,16,128]{2,1,0:T(8,128)S(1)} %broadcast_select_fusion.2), channel_id=1, source_target_pairs={{32,0},{64,32},{96,64},{33,1},{65,33},{97,65},{34,2},{66,34},{98,6... | collective-permute-start | bytes 122888 | tf_op jit(solution)/shard_map/ppermute | solution.py:351
  6.0 6.4 %collective-permute-start = (f32[5,16,128]{2,1,0:T(8,128)S(1)}, f32[5,16,128]{2,1,0:T(8,128)S(1)}, u32[]{:S(2)}, u32[]{:S(2)}) collective-permute-start(f32[5,16,128]{2,1,0:T(8,128)S(1)} %broadcast_select_fusion.3), channel_id=1, source_target_pairs={{0,32},{32,64},{64,96},{1,33},{33,65},{65,97},{2,34},{34,66},{66,9... | collective-permute-start | bytes 122888 | tf_op jit(solution)/shard_map/ppermute | solution.py:351
  12.5 6.9 %collective-permute-start.2 = (f32[5,40,128]{2,1,0:T(8,128)S(1)}, f32[5,40,128]{2,1,0:T(8,128)S(1)}, u32[]{:S(2)}, u32[]{:S(2)}) collective-permute-start(f32[5,40,128]{2,1,0:T(8,128)S(1)} %pad_maximum_fusion), channel_id=1, source_target_pairs={{0,1},{1,2},{2,3},{3,4},{4,5},{5,6},{6,7},{7,8},{8,9},{9,10},{10,1... | collective-permute-start | bytes 307208 | tf_op jit(solution)/shard_map/ppermute | solution.py:351
  17.5 6.0 %collective-permute-start.3 = (f32[5,40,128]{2,1,0:T(8,128)S(1)}, f32[5,40,128]{2,1,0:T(8,128)S(1)}, u32[]{:S(2)}, u32[]{:S(2)}) collective-permute-start(f32[5,40,128]{2,1,0:T(8,128)S(1)} %pad_maximum_fusion.1), channel_id=1, source_target_pairs={{1,0},{2,1},{3,2},{4,3},{5,4},{6,5},{7,6},{8,7},{9,8},{10,9},{11,1... | collective-permute-start | bytes 307208 | tf_op jit(solution)/shard_map/ppermute | solution.py:351
  23.4 1.0 copy-start
  24.4 0.9 copy-start.1
  32.2 5.1 %collective-permute-start.4 = (f32[5,16,128]{2,1,0:T(8,128)S(1)}, f32[5,16,128]{2,1,0:T(8,128)S(1)}, u32[]{:S(2)}, u32[]{:S(2)}) collective-permute-start(f32[5,16,128]{2,1,0:T(8,128)S(1)} %get-tuple-element.11), channel_id=1, source_target_pairs={{0,32},{32,64},{64,96},{1,33},{33,65},{65,97},{2,34},{34,66},{66,9... | collective-permute-start | bytes 122888 | tf_op jit(solution)/shard_map/ppermute | solution.py:351
  36.0 4.7 %collective-permute-start.5 = (f32[5,16,128]{2,1,0:T(8,128)S(1)}, f32[5,16,128]{2,1,0:T(8,128)S(1)}, u32[]{:S(2)}, u32[]{:S(2)}) collective-permute-start(f32[5,16,128]{2,1,0:T(8,128)S(1)} %get-tuple-element.12), channel_id=1, source_target_pairs={{32,0},{64,32},{96,64},{33,1},{65,33},{97,65},{34,2},{66,34},{98,6... | collective-permute-start | bytes 122888 | tf_op jit(solution)/shard_map/ppermute | solution.py:351
  40.8 5.3 %collective-permute-start.6 = (f32[5,40,128]{2,1,0:T(8,128)S(1)}, f32[5,40,128]{2,1,0:T(8,128)S(1)}, u32[]{:S(2)}, u32[]{:S(2)}) collective-permute-start(f32[5,40,128]{2,1,0:T(8,128)S(1)} %pad_maximum_fusion.2), channel_id=1, source_target_pairs={{0,1},{1,2},{2,3},{3,4},{4,5},{5,6},{6,7},{7,8},{8,9},{9,10},{10,1... | collective-permute-start | bytes 307208 | tf_op jit(solution)/shard_map/ppermute | solution.py:351
  44.2 6.0 %collective-permute-start.7 = (f32[5,40,128]{2,1,0:T(8,128)S(1)}, f32[5,40,128]{2,1,0:T(8,128)S(1)}, u32[]{:S(2)}, u32[]{:S(2)}) collective-permute-start(f32[5,40,128]{2,1,0:T(8,128)S(1)} %pad_maximum_fusion.3), channel_id=1, source_target_pairs={{1,0},{2,1},{3,2},{4,3},{5,4},{6,5},{7,6},{8,7},{9,8},{10,9},{11,1... | collective-permute-start | bytes 307208 | tf_op jit(solution)/shard_map/ppermute | solution.py:351

commit v2 on v1

--- a/solution.py
+++ b/solution.py
@@ -124,20 +124,37 @@
     return y_row
 
 
-def step_one_kernel(pops, solid, wetting, xlo, xhi, ylo, yhi, out, xup, xdn, yup, ydn, f, mark, res, sem_in, sem_out):
+def prep_kernel(pops, solid, wetting, mark, xup, xdn, yup, ydn, x_planes, y_tiles, sem_x, sem_y):
+    copies = []
+    for k in range(5):
+        copies.append(pltpu.make_async_copy(pops.at[X_UP[k], XS - 1], x_planes.at[k], sem_x.at[k]))
+        copies.append(pltpu.make_async_copy(pops.at[X_DOWN[k], 0], x_planes.at[5 + k], sem_x.at[5 + k]))
+        copies.append(pltpu.make_async_copy(pops.at[Y_UP[k], :, 8:16], y_tiles.at[k], sem_y.at[k]))
+        copies.append(pltpu.make_async_copy(pops.at[Y_DOWN[k], :, 0:8], y_tiles.at[5 + k], sem_y.at[5 + k]))
+    for copy in copies:
+        copy.start()
+    clear = jnp.zeros((YS, ZS), jnp.float32)
+    mark[0] = clear
+    mark[XS + 1] = clear
+    for x in range(XS):
+        mark[x + 1] = jnp.where(solid[x] == 1, jnp.where(wetting[x] == 1, -BIG, BIG), 0.0)
+    for copy in copies:
+        copy.wait()
+    for k in range(5):
+        for out, at, x in ((xup, k, XS), (xdn, 5 + k, 1)):
+            m = mark[x]
+            out[k] = jnp.where(m == 0.0, x_planes[at], m)
+    for out, first, y in ((yup, 0, 7), (ydn, 5, 0)):
+        m = mark[1 : XS + 1, y + (8 if first == 0 else 0), :]
+        for k in range(5):
+            out[k, 1 : XS + 1, :] = jnp.where(m == 0.0, y_tiles[first + k, :, y, :], m)
+
+
+def step_one_kernel(pops, mark, xlo, xhi, ylo, yhi, out, xup, xdn, yup, ydn, f, res, sem_in, sem_out):
     copies = fetch(pops, f, sem_in)
     for copy in copies:
         copy.start()
     place_x_halo(f, xlo, xhi)
-    mark[0] = jnp.zeros((YS, ZS), jnp.float32)
-    mark[XS + 1] = jnp.zeros((YS, ZS), jnp.float32)
-
-    def marks(x, carry):
-        mark[x + 1] = jnp.where(solid[x] == 1, jnp.where(wetting[x] == 1, -BIG, BIG), 0.0)
-        return carry
-
-    lax.fori_loop(0, XS, marks, 0)
-
     def plane(x, carry):
         marked = {c: mark[x + 1 - c] for c in (-1, 0, 1)}
 
@@ -288,22 +305,41 @@
     return pltpu.CompilerParams(vmem_limit_bytes=48 * 1024 * 1024)
 
 
-def step_one(pops, solid, wetting, halo):
+EDGES = (sds(5, YS, ZS), sds(5, YS, ZS), sds(5, HALO_ROWS, ZS), sds(5, HALO_ROWS, ZS))
+
+
+def prep(pops, solid, wetting):
+    return pl.pallas_call(
+        prep_kernel,
+        out_shape=(sds(XS + 2, YS, ZS), *EDGES),
+        in_specs=[ANY, VMEM, VMEM],
+        out_specs=(VMEM,) * 5,
+        scratch_shapes=[
+            pltpu.VMEM((10, YS, ZS), jnp.float32),
+            pltpu.VMEM((10, XS, 8, ZS), jnp.float32),
+            pltpu.SemaphoreType.DMA((10,)),
+            pltpu.SemaphoreType.DMA((10,)),
+        ],
+        compiler_params=params(),
+        name="prep",
+    )(pops, solid, wetting)
+
+
+def step_one(pops, mark, halo):
     return pl.pallas_call(
         step_one_kernel,
-        out_shape=(sds(19, XS, YS, ZS), sds(5, YS, ZS), sds(5, YS, ZS), sds(5, HALO_ROWS, ZS), sds(5, HALO_ROWS, ZS)),
-        in_specs=[ANY] + [VMEM] * 6,
+        out_shape=(sds(19, XS, YS, ZS), *EDGES),
+        in_specs=[ANY] + [VMEM] * 5,
         out_specs=(ANY, VMEM, VMEM, VMEM, VMEM),
         scratch_shapes=[
             pltpu.VMEM((19, XS + 2, YS, ZS), jnp.float32),
-            pltpu.VMEM((XS + 2, YS, ZS), jnp.float32),
             pltpu.VMEM((19, XS, YS, ZS), jnp.float32),
             pltpu.SemaphoreType.DMA((CHUNKS,)),
             pltpu.SemaphoreType.DMA((CHUNKS,)),
         ],
         compiler_params=params(),
         name="step_one",
-    )(pops, solid, wetting, *halo)
+    )(pops, mark, *halo)
 
 
 def step_two(owners, f1, halo, peers):
@@ -347,7 +383,7 @@
 
 def shift(value, axis, up):
     count = lax.axis_size(axis)
-    steps = [(i, i + 1) if up else (i + 1, i) for i in range(count - 1)]
+    steps = [(i, (i + 1) % count) if up else ((i + 1) % count, i) for i in range(count)]
     return lax.ppermute(value, axis, steps)
 
 
@@ -375,21 +411,8 @@
 
 def per_device(populations, solid, wetting, dest):
     peers = lax.axis_size("blk")
-    mark = jnp.where(solid == 1, jnp.where(wetting == 1, -BIG, BIG), 0.0)
-
-    def marked(channels, x, y):
-        m = mark[x, y]
-        return jnp.where(m == 0.0, jnp.stack([populations[i, x, y] for i in channels]), m)
-
-    every = slice(None)
-    grow = ((0, 0), (1, HALO_ROWS - XS - 1), (0, 0))
-    halo = exchange(
-        marked(X_UP, XS - 1, every),
-        marked(X_DOWN, 0, every),
-        jnp.pad(marked(Y_UP, every, YS - 1), grow),
-        jnp.pad(marked(Y_DOWN, every, 0), grow),
-    )
-    f1, *edges = step_one(populations, solid, wetting, halo)
+    mark, *edges = prep(populations, solid, wetting)
+    f1, *edges = step_one(populations, mark, exchange(*edges))
     outgoing = step_two(dest[0] // BLOCKS, f1, exchange(*edges), peers)
     incoming = lax.all_to_all(outgoing, "blk", split_axis=0, concat_axis=0, tiled=True)
     return place(incoming).transpose(1, 0, 2)

time: 194 us -> 179 us (0.923)
  starting transfers between devices: 23 us -> 13.1 us
  local copies, waits for them, and re-layouts: 7.06 us -> 4.33 us
  waiting for transfers between devices: 11.5 us -> 9.45 us
    ppermute x8, starting transfers between devices: 23 us -> 13.1 us  [shift(): return lax.ppermute(value, axis, steps)]
    ppermute x8, waiting for transfers between devices: 11.5 us -> 9.45 us  [shift(): return lax.ppermute(value, axis, steps)]
    pallas_call x1 -> x2, Pallas kernels: 6.81 us -> 7.43 us  [the longest x1 6.81 us: step_one(): pl.pallas_call(step_one_kernel, out_shape=(sds(19, XS, YS, ZS), *EDGES),...]
    unnamed x18 -> x8, local copies, waits for them, and re-layouts: 4.8 us -> 4.32 us
  transfers between devices with their start and end apart: 8 -> 8, of which waited for: 3 -> 8; matrix products, arithmetic and copies ran while one was open for 1% -> 0% of each run, Pallas kernels for 0% -> 0%
where the time goes in v2:
time: 179 us; the launch traced here: 178 us
  blocking collectives  126 us (70%)
  Pallas kernels  25.2 us (14%)
  starting transfers between devices  13.1 us (7%)
  waiting for transfers between devices  9.45 us (5%)
  local copies, waits for them, and re-layouts  4.33 us (2%)
    all_to_all x1, blocking collectives, per_device(): lax.all_to_all(outgoing, 'blk', split_axis=0, concat_axis=0, tiled=True)  126 us
    ppermute x8, starting transfers between devices, shift(): return lax.ppermute(value, axis, steps)  13.1 us
    pallas_call x1, Pallas kernels, step_two(): pl.pallas_call(step_two_kernel, out_shape=sds(peers, SLOT_ROWS, ZS), in_s...  12.5 us
    ppermute x8, waiting for transfers between devices, shift(): return lax.ppermute(value, axis, steps)  9.45 us
    pallas_call x1, Pallas kernels, step_one(): pl.pallas_call(step_one_kernel, out_shape=(sds(19, XS, YS, ZS), *EDGES),...  6.81 us
    pallas_call x1, Pallas kernels, place(): pl.pallas_call(place_kernel, out_shape=sds(19, BLOCKS, 4096), in_specs=[A...  5.23 us
    unnamed x8, local copies, waits for them, and re-layouts  4.32 us
  transfers between devices with their start and end apart: 8, of which 8 were waited for; matrix products, arithmetic and copies ran while one was open for 0% of the time, Pallas kernels for 0%

profile of v2, /device:TPU:1, one launch (start us, length us, event | category | flops | bytes accessed | tf_op | source)
XLA Modules:
  0.0 178.3 jit_solution(1052511687388418431)
XLA Ops:
  0.0 0.0 copy-start
  0.0 2.4 %copy-done = f32[19,32,16,128]{3,2,1,0:T(8,128)S(1)} copy-done((f32[19,32,16,128]{3,2,1,0:T(8,128)S(1)}, f32[19,32,16,128]{3,2,1,0:T(8,128)}, u32[]{:S(2)}) %copy-start) | copy-done | bytes 4980760
  2.4 0.0 copy-start.1
  2.4 0.9 copy-done.1
  3.4 0.9 copy-done.2
  4.3 0.6 prep.1
  4.9 0.0 copy-start.3
  4.9 2.1 %collective-permute-start = (f32[5,16,128]{2,1,0:T(8,128)S(1)}, f32[5,16,128]{2,1,0:T(8,128)S(1)}, u32[]{:S(2)}, u32[]{:S(2)}) collective-permute-start(f32[5,16,128]{2,1,0:T(8,128)S(1)} %get-tuple-element.16), channel_id=1, source_target_pairs={{0,32},{32,64},{64,96},{96,0},{1,33},{33,65},{65,97},{97,1},{2,34}... | collective-permute-start | bytes 122888 | tf_op jit(solution)/shard_map/ppermute | solution.py:387
  7.1 1.3 collective-permute-start.1
  8.4 1.3 collective-permute-done.xlo
  9.7 0.2 collective-permute-done.1.xhi
  9.9 0.1 fusion.11
  10.0 3.7 %collective-permute-start.2 = (f32[5,40,128]{2,1,0:T(8,128)S(1)}, f32[5,40,128]{2,1,0:T(8,128)S(1)}, u32[]{:S(2)}, u32[]{:S(2)}) collective-permute-start(f32[5,40,128]{2,1,0:T(8,128)S(1)} %pad_maximum_fusion), channel_id=1, source_target_pairs={{0,1},{1,2},{2,3},{3,4},{4,5},{5,6},{6,7},{7,8},{8,9},{9,10},{10,1... | collective-permute-start | bytes 307208 | tf_op jit(solution)/shard_map/ppermute | solution.py:387
  13.7 0.1 fusion.10
  13.8 0.1 collective-permute-start.3
  13.9 1.5 collective-permute-done.2.ylo
  15.4 2.9 %collective-permute-done.3.yhi = f32[5,40,128]{2,1,0:T(8,128)S(1)} collective-permute-done((f32[5,40,128]{2,1,0:T(8,128)S(1)}, f32[5,40,128]{2,1,0:T(8,128)S(1)}, u32[]{:S(2)}, u32[]{:S(2)}) %collective-permute-start.3) | collective-permute-done | bytes 102432 | tf_op jit(solution)/shard_map/ppermute | solution.py:387
  18.3 6.8 %step_one.1 = (f32[19,32,16,128]{3,2,1,0:T(8,128)S(1)}, f32[5,16,128]{2,1,0:T(8,128)S(1)}, f32[5,16,128]{2,1,0:T(8,128)S(1)}, f32[5,40,128]{2,1,0:T(8,128)S(1)}, f32[5,40,128]{2,1,0:T(8,128)S(1)}) custom-call(f32[19,32,16,128]{3,2,1,0:T(8,128)} %pops.3, f32[34,16,128]{2,1,0:T(8,128)S(1)} %get-tuple-element.15.mark, ...), custom_call_target="tpu_custom_call" | custom-call | tf_op jit(solution)/shard_map/step_one/pallas_call | solution.py:329
  25.1 1.3 collective-permute-start.4
  26.4 1.6 collective-permute-start.5
  27.9 1.3 collective-permute-done.4.xlo
  29.2 0.1 collective-permute-done.5.xhi
  29.3 0.1 fusion.9
  29.4 1.1 collective-permute-start.6
  30.5 0.1 fusion.8
  30.6 1.9 %collective-permute-start.7 = (f32[5,40,128]{2,1,0:T(8,128)S(1)}, f32[5,40,128]{2,1,0:T(8,128)S(1)}, u32[]{:S(2)}, u32[]{:S(2)}) collective-permute-start(f32[5,40,128]{2,1,0:T(8,128)S(1)} %pad_maximum_fusion.3), channel_id=1, source_target_pairs={{1,0},{2,1},{3,2},{4,3},{5,4},{6,5},{7,6},{8,7},{9,8},{10,9},{11,1... | collective-permute-start | bytes 307208 | tf_op jit(solution)/shard_map/ppermute | solution.py:387
  32.5 0.0 copy-done.3
  32.5 0.6 collective-permute-done.6.ylo
  33.1 1.7 collective-permute-done.7.yhi
  34.8 12.5 %step_two.1 = f32[32,616,128]{2,1,0:T(8,128)} custom-call(s32[16]{0:T(128)S(1)} %and_select_fusion.owners, f32[19,32,16,128]{3,2,1,0:T(8,128)S(1)} %get-tuple-element.20.f1, f32[5,16,128]{2,1,0:T(8,128)S(1)} %collective-permute-done.4.xlo, f32[5,16,128]{2,1,0:T(8,128)S(1)} %collective-permute-done.5.xhi, f32[5,40,128]{2,1,0:T(8,128)S(1)} %collective-permute-done.6.ylo, ...), custom_call_target="tpu_custom_call" | custom-call | tf_op jit(solution)/shard_map/step_two/pallas_call | solution.py:346
  47.3 125.8 %all_to_all.5.incoming = f32[32,616,128]{2,1,0:T(8,128)} all-to-all(f32[32,616,128]{2,1,0:T(8,128)} %step_two.1), channel_id=1, replica_groups=mesh['slab'=4,'blk'=32] {'blk'}, dimensions={0} | all-to-all | bytes 20185088 | tf_op jit(solution)/shard_map/all_to_all | solution.py:417
  173.1 5.2 %place.1 = f32[19,16,4096]{2,1,0:T(8,128)} custom-call(f32[32,616,128]{2,1,0:T(8,128)} %all_to_all.5.incoming), custom_call_target="tpu_custom_call" | custom-call | tf_op jit(solution)/shard_map/place/pallas_call | solution.py:366
  (15 shorter events, 0.1 us)
Async XLA Ops:
  0.0 2.4 %copy-start = (f32[19,32,16,128]{3,2,1,0:T(8,128)S(1)}, f32[19,32,16,128]{3,2,1,0:T(8,128)}, u32[]{:S(2)}) copy-start(f32[19,32,16,128]{3,2,1,0:T(8,128)} %pops.3) | copy-start | bytes 14942212
  2.4 0.9 copy-start.1
  3.4 0.9 copy-start.2
  4.9 27.6 %copy-start.3 = (s32[1,16]{1,0:T(1,128)S(1)}, s32[1,16]{1,0:T(1,128)}, u32[]{:S(2)}) copy-start(s32[1,16]{1,0:T(1,128)} %param.7) | copy-start | bytes 196
  4.9 4.8 %collective-permute-start = (f32[5,16,128]{2,1,0:T(8,128)S(1)}, f32[5,16,128]{2,1,0:T(8,128)S(1)}, u32[]{:S(2)}, u32[]{:S(2)}) collective-permute-start(f32[5,16,128]{2,1,0:T(8,128)S(1)} %get-tuple-element.16), channel_id=1, source_target_pairs={{0,32},{32,64},{64,96},{96,0},{1,33},{33,65},{65,97},{97,1},{2,34}... | collective-permute-start | bytes 122888 | tf_op jit(solution)/shard_map/ppermute | solution.py:387
  7.1 2.9 %collective-permute-start.1 = (f32[5,16,128]{2,1,0:T(8,128)S(1)}, f32[5,16,128]{2,1,0:T(8,128)S(1)}, u32[]{:S(2)}, u32[]{:S(2)}) collective-permute-start(f32[5,16,128]{2,1,0:T(8,128)S(1)} %get-tuple-element.17), channel_id=1, source_target_pairs={{32,0},{64,32},{96,64},{0,96},{33,1},{65,33},{97,65},{1,97},{34,2}... | collective-permute-start | bytes 122888 | tf_op jit(solution)/shard_map/ppermute | solution.py:387
  10.0 5.4 %collective-permute-start.2 = (f32[5,40,128]{2,1,0:T(8,128)S(1)}, f32[5,40,128]{2,1,0:T(8,128)S(1)}, u32[]{:S(2)}, u32[]{:S(2)}) collective-permute-start(f32[5,40,128]{2,1,0:T(8,128)S(1)} %pad_maximum_fusion), channel_id=1, source_target_pairs={{0,1},{1,2},{2,3},{3,4},{4,5},{5,6},{6,7},{7,8},{8,9},{9,10},{10,1... | collective-permute-start | bytes 307208 | tf_op jit(solution)/shard_map/ppermute | solution.py:387
  13.8 4.4 %collective-permute-start.3 = (f32[5,40,128]{2,1,0:T(8,128)S(1)}, f32[5,40,128]{2,1,0:T(8,128)S(1)}, u32[]{:S(2)}, u32[]{:S(2)}) collective-permute-start(f32[5,40,128]{2,1,0:T(8,128)S(1)} %pad_maximum_fusion.1), channel_id=1, source_target_pairs={{1,0},{2,1},{3,2},{4,3},{5,4},{6,5},{7,6},{8,7},{9,8},{10,9},{11,1... | collective-permute-start | bytes 307208 | tf_op jit(solution)/shard_map/ppermute | solution.py:387
  25.1 4.1 %collective-permute-start.4 = (f32[5,16,128]{2,1,0:T(8,128)S(1)}, f32[5,16,128]{2,1,0:T(8,128)S(1)}, u32[]{:S(2)}, u32[]{:S(2)}) collective-permute-start(f32[5,16,128]{2,1,0:T(8,128)S(1)} %get-tuple-element.21), channel_id=1, source_target_pairs={{0,32},{32,64},{64,96},{96,0},{1,33},{33,65},{65,97},{97,1},{2,34}... | collective-permute-start | bytes 122888 | tf_op jit(solution)/shard_map/ppermute | solution.py:387
  26.4 2.9 %collective-permute-start.5 = (f32[5,16,128]{2,1,0:T(8,128)S(1)}, f32[5,16,128]{2,1,0:T(8,128)S(1)}, u32[]{:S(2)}, u32[]{:S(2)}) collective-permute-start(f32[5,16,128]{2,1,0:T(8,128)S(1)} %get-tuple-element.22), channel_id=1, source_target_pairs={{32,0},{64,32},{96,64},{0,96},{33,1},{65,33},{97,65},{1,97},{34,2}... | collective-permute-start | bytes 122888 | tf_op jit(solution)/shard_map/ppermute | solution.py:387
  29.4 3.7 %collective-permute-start.6 = (f32[5,40,128]{2,1,0:T(8,128)S(1)}, f32[5,40,128]{2,1,0:T(8,128)S(1)}, u32[]{:S(2)}, u32[]{:S(2)}) collective-permute-start(f32[5,40,128]{2,1,0:T(8,128)S(1)} %pad_maximum_fusion.2), channel_id=1, source_target_pairs={{0,1},{1,2},{2,3},{3,4},{4,5},{5,6},{6,7},{7,8},{8,9},{9,10},{10,1... | collective-permute-start | bytes 307208 | tf_op jit(solution)/shard_map/ppermute | solution.py:387
  30.6 4.2 %collective-permute-start.7 = (f32[5,40,128]{2,1,0:T(8,128)S(1)}, f32[5,40,128]{2,1,0:T(8,128)S(1)}, u32[]{:S(2)}, u32[]{:S(2)}) collective-permute-start(f32[5,40,128]{2,1,0:T(8,128)S(1)} %pad_maximum_fusion.3), channel_id=1, source_target_pairs={{1,0},{2,1},{3,2},{4,3},{5,4},{6,5},{7,6},{8,7},{9,8},{10,9},{11,1... | collective-permute-start | bytes 307208 | tf_op jit(solution)/shard_map/ppermute | solution.py:387

commit v3 on v2

--- a/solution.py
+++ b/solution.py
@@ -31,6 +31,7 @@
 BLOCKS = 16
 BLOCK_ROWS = 19 * 32
 SLOT_ROWS = BLOCK_ROWS + 8
+PARTS = ((0, 10), (10, 19))
 
 
 def collide(f):
@@ -124,7 +125,13 @@
     return y_row
 
 
-def prep_kernel(pops, solid, wetting, mark, xup, xdn, yup, ydn, x_planes, y_tiles, sem_x, sem_y):
+def prep_kernel(pops, solid_in, wetting_in, mark, xup, xdn, yup, ydn, x_planes, y_tiles, solid, wetting, sem_x, sem_y, sem_k):
+    kinds = [
+        pltpu.make_async_copy(solid_in, solid, sem_k.at[0]),
+        pltpu.make_async_copy(wetting_in, wetting, sem_k.at[1]),
+    ]
+    for copy in kinds:
+        copy.start()
     copies = []
     for k in range(5):
         copies.append(pltpu.make_async_copy(pops.at[X_UP[k], XS - 1], x_planes.at[k], sem_x.at[k]))
@@ -136,6 +143,8 @@
     clear = jnp.zeros((YS, ZS), jnp.float32)
     mark[0] = clear
     mark[XS + 1] = clear
+    for copy in kinds:
+        copy.wait()
     for x in range(XS):
         mark[x + 1] = jnp.where(solid[x] == 1, jnp.where(wetting[x] == 1, -BIG, BIG), 0.0)
     for copy in copies:
@@ -150,7 +159,9 @@
             out[k, 1 : XS + 1, :] = jnp.where(m == 0.0, y_tiles[first + k, :, y, :], m)
 
 
-def step_one_kernel(pops, mark, xlo, xhi, ylo, yhi, out, xup, xdn, yup, ydn, f, res, sem_in, sem_out):
+def step_one_kernel(pops, mark_in, xlo, xhi, ylo, yhi, out, xup, xdn, yup, ydn, f, mark, res, sem_mark, sem_in, sem_out):
+    mark_copy = pltpu.make_async_copy(mark_in, mark, sem_mark)
+    mark_copy.start()
     copies = fetch(pops, f, sem_in)
     for copy in copies:
         copy.start()
@@ -175,11 +186,12 @@
         return carry
 
     outs = []
+    mark_copy.wait()
     copies[0].wait()
     for c in range(CHUNKS):
         if c + 1 < CHUNKS:
             copies[c + 1].wait()
-        lax.fori_loop(c * CHUNK, (c + 1) * CHUNK, plane, 0)
+        lax.fori_loop(c * CHUNK, (c + 1) * CHUNK, plane, 0, unroll=2)
         at = pl.ds(c * CHUNK, CHUNK)
         outs.append(pltpu.make_async_copy(res.at[:, at], out.at[:, at], sem_out.at[c]))
         outs[-1].start()
@@ -220,13 +232,15 @@
         )
         fluid = jnp.abs(f[0, x + 1]) < HALF_BIG
         base = x // 16 * (8 * SLOT_ROWS) + x % 16 * 2
+        tiles = []
         for i in range(19):
             value = jnp.where(fluid, new[i], 0.0)
-            for half in range(2):
-                v = pltpu.roll(value[half * 8 : half * 8 + 8], 0, 1, stride=16, stride_axis=0)
-                v = jnp.take_along_axis(v, pick, axis=0)
-                v = pltpu.roll(v, 16, 1, stride=16, stride_axis=0)
-                buf[pl.ds(base + i * 32 + half, 8, stride=SLOT_ROWS + 1), :] = v
+            tiles += [(i * 32 + half, value[half * 8 : half * 8 + 8]) for half in range(2)]
+        tiles = [(at, pltpu.roll(v, 0, 1, stride=16, stride_axis=0)) for at, v in tiles]
+        tiles = [(at, jnp.take_along_axis(v, pick, axis=0)) for at, v in tiles]
+        tiles = [(at, pltpu.roll(v, 16, 1, stride=16, stride_axis=0)) for at, v in tiles]
+        for at, v in tiles:
+            buf[pl.ds(base + at, 8, stride=SLOT_ROWS), :] = v
         return carry
 
     outs = []
@@ -234,7 +248,7 @@
     for c in range(CHUNKS):
         if c + 1 < CHUNKS:
             copies[c + 1].wait()
-        lax.fori_loop(c * CHUNK, (c + 1) * CHUNK, plane, 0)
+        lax.fori_loop(c * CHUNK, (c + 1) * CHUNK, plane, 0, unroll=2)
         if c == 0:
             for clear in clears:
                 clear.wait()
@@ -261,33 +275,38 @@
     found = jnp.zeros((1, ZS), jnp.int32)
     for p in range(peers):
         found += jnp.where(labels[p, 7:8, :] == slot, p, 0)
+    found = jnp.clip(found, 0, peers - 1)
+    sources = [found[0, k] for k in range(BLOCKS)]
     ins = []
-    for k in range(BLOCKS):
-        source = jnp.clip(jnp.sum(jnp.where(lane == k, found, 0)), 0, peers - 1)
-        ins.append(
-            pltpu.make_async_copy(
-                incoming.at[source], blocks.at[pl.ds(k * SLOT_ROWS, SLOT_ROWS)], sem_in.at[k]
+    for part, (low, high) in enumerate(PARTS):
+        for k in range(BLOCKS):
+            rows = (high - low) * 32
+            ins.append(
+                pltpu.make_async_copy(
+                    incoming.at[sources[k], pl.ds(low * 32, rows)],
+                    blocks.at[pl.ds(k * SLOT_ROWS + low * 32, rows)],
+                    sem_in.at[part * BLOCKS + k],
+                )
             )
-        )
-        ins[-1].start()
+            ins[-1].start()
     outs = []
-    for h in range(2):
-        for k in range(8):
-            ins[h * 8 + k].wait()
-
-        def channel(i, carry):
+
+    def channel(i, carry):
+        for h in range(2):
             for j in range(32):
-                at = h * 8 * SLOT_ROWS + 7 + i * 32 + j
+                at = h * 8 * SLOT_ROWS + i * 32 + j
                 res[i, h * 8 : h * 8 + 8, j * 128 : (j + 1) * 128] = blocks[
-                    pl.ds(at, 8, stride=SLOT_ROWS - 1), :
+                    pl.ds(at, 8, stride=SLOT_ROWS), :
                 ]
-            return carry
-
-        for part, (low, high) in enumerate(((0, 5), (5, 10), (10, 15), (15, 19))):
-            lax.fori_loop(low, high, channel, 0)
-            at = (pl.ds(low, high - low), pl.ds(h * 8, 8))
-            outs.append(pltpu.make_async_copy(res.at[at], out.at[at], sem_out.at[h * 4 + part]))
-            outs[-1].start()
+        return carry
+
+    for part, (low, high) in enumerate(PARTS):
+        for k in range(BLOCKS):
+            ins[part * BLOCKS + k].wait()
+        lax.fori_loop(low, high, channel, 0)
+        at = pl.ds(low, high - low)
+        outs.append(pltpu.make_async_copy(res.at[at], out.at[at], sem_out.at[part]))
+        outs[-1].start()
     for copy in outs:
         copy.wait()
 
@@ -301,8 +320,8 @@
     return jax.ShapeDtypeStruct(shape, jnp.float32)
 
 
-def params():
-    return pltpu.CompilerParams(vmem_limit_bytes=48 * 1024 * 1024)
+def params(mib=48):
+    return pltpu.CompilerParams(vmem_limit_bytes=mib * 1024 * 1024)
 
 
 EDGES = (sds(5, YS, ZS), sds(5, YS, ZS), sds(5, HALO_ROWS, ZS), sds(5, HALO_ROWS, ZS))
@@ -312,15 +331,18 @@
     return pl.pallas_call(
         prep_kernel,
         out_shape=(sds(XS + 2, YS, ZS), *EDGES),
-        in_specs=[ANY, VMEM, VMEM],
+        in_specs=[ANY, ANY, ANY],
         out_specs=(VMEM,) * 5,
         scratch_shapes=[
             pltpu.VMEM((10, YS, ZS), jnp.float32),
             pltpu.VMEM((10, XS, 8, ZS), jnp.float32),
+            pltpu.VMEM((XS, YS, ZS), jnp.int32),
+            pltpu.VMEM((XS, YS, ZS), jnp.int32),
             pltpu.SemaphoreType.DMA((10,)),
             pltpu.SemaphoreType.DMA((10,)),
+            pltpu.SemaphoreType.DMA((2,)),
         ],
-        compiler_params=params(),
+        compiler_params=params(60),
         name="prep",
     )(pops, solid, wetting)
 
@@ -329,11 +351,13 @@
     return pl.pallas_call(
         step_one_kernel,
         out_shape=(sds(19, XS, YS, ZS), *EDGES),
-        in_specs=[ANY] + [VMEM] * 5,
+        in_specs=[ANY, ANY] + [VMEM] * 4,
         out_specs=(ANY, VMEM, VMEM, VMEM, VMEM),
         scratch_shapes=[
             pltpu.VMEM((19, XS + 2, YS, ZS), jnp.float32),
+            pltpu.VMEM((XS + 2, YS, ZS), jnp.float32),
             pltpu.VMEM((19, XS, YS, ZS), jnp.float32),
+            pltpu.SemaphoreType.DMA,
             pltpu.SemaphoreType.DMA((CHUNKS,)),
             pltpu.SemaphoreType.DMA((CHUNKS,)),
         ],
@@ -373,8 +397,8 @@
             pltpu.VMEM((BLOCKS * SLOT_ROWS, ZS), jnp.float32),
             pltpu.VMEM((19, BLOCKS, 4096), jnp.float32),
             pltpu.SemaphoreType.DMA,
-            pltpu.SemaphoreType.DMA((BLOCKS,)),
-            pltpu.SemaphoreType.DMA((8,)),
+            pltpu.SemaphoreType.DMA((len(PARTS) * BLOCKS,)),
+            pltpu.SemaphoreType.DMA((len(PARTS),)),
         ],
         compiler_params=params(),
         name="place",

time: 179 us -> 175 us (0.978)
  Pallas kernels: 25.2 us -> 23 us
  local copies, waits for them, and re-layouts: 4.33 us -> 2.53 us
    pallas_call x1, Pallas kernels: 12.5 us -> 8.88 us  [step_two(): pl.pallas_call(step_two_kernel, out_shape=sds(peers, SLOT_ROWS, ZS), in_s...]
    unnamed x8 -> x4, local copies, waits for them, and re-layouts: 4.32 us -> 0.96 us
    pallas_call x1, Pallas kernels: 0.62 us -> 2.65 us  [prep(): pl.pallas_call(prep_kernel, out_shape=(sds(XS + 2, YS, ZS), *EDGES), in_s...]
  transfers between devices with their start and end apart: 8 -> 8, of which waited for: 8 -> 7; matrix products, arithmetic and copies ran while one was open for 0% -> 1% of each run, Pallas kernels for 0% -> 0%
where the time goes in v3:
time: 175 us
  blocking collectives  126 us (72%)
  Pallas kernels  23 us (13%)
  starting transfers between devices  13.1 us (7%)
  waiting for transfers between devices  8.12 us (5%)
  local copies, waits for them, and re-layouts  2.53 us (1%)
  other arithmetic  1.9 us (1%)
    all_to_all x1, blocking collectives, per_device(): lax.all_to_all(outgoing, 'blk', split_axis=0, concat_axis=0, tiled=True)  126 us
    ppermute x8, starting transfers between devices, shift(): return lax.ppermute(value, axis, steps)  13.1 us
    pallas_call x1, Pallas kernels, step_two(): pl.pallas_call(step_two_kernel, out_shape=sds(peers, SLOT_ROWS, ZS), in_s...  8.88 us
    ppermute x8, waiting for transfers between devices, shift(): return lax.ppermute(value, axis, steps)  8.12 us
    pallas_call x1, Pallas kernels, place(): pl.pallas_call(place_kernel, out_shape=sds(19, BLOCKS, 4096), in_specs=[A...  5.86 us
    pallas_call x1, Pallas kernels, step_one(): pl.pallas_call(step_one_kernel, out_shape=(sds(19, XS, YS, ZS), *EDGES),...  5.59 us
  transfers between devices with their start and end apart: 8, of which 7 were waited for; matrix products, arithmetic and copies ran while one was open for 1% of the time, Pallas kernels for 0%

profile of v3, /device:TPU:1, one launch (start us, length us, event | category | flops | bytes accessed | tf_op | source)
XLA Modules:
  0.0 174.6 jit_solution(1990830293571025549)
XLA Ops:
  0.0 2.7 %prep.1 = (f32[34,16,128]{2,1,0:T(8,128)}, f32[5,16,128]{2,1,0:T(8,128)}, f32[5,16,128]{2,1,0:T(8,128)}, f32[5,40,128]{2,1,0:T(8,128)}, f32[5,40,128]{2,1,0:T(8,128)}) custom-call(f32[19,32,16,128]{3,2,1,0:T(8,128)} %pops.3, s32[32,16,128]{2,1,0:T(8,128)} %solid_in.1, s32[32,16,128]{2,1,0:T(8,128)} %wetting_in.1), custom_call_target="tpu_custom_call" | custom-call | tf_op jit(solution)/shard_map/prep/pallas_call | solution.py:331
  2.7 0.0 copy-start.1
  2.7 2.1 %collective-permute-start = (f32[5,16,128]{2,1,0:T(8,128)}, f32[5,16,128]{2,1,0:T(8,128)S(1)}, u32[]{:S(2)}, u32[]{:S(2)}) collective-permute-start(f32[5,16,128]{2,1,0:T(8,128)} %get-tuple-element.16), channel_id=1, source_target_pairs={{0,32},{32,64},{64,96},{96,0},{1,33},{33,65},{65,97},{97,1},{2,34}... | collective-permute-start | bytes 122888 | tf_op jit(solution)/shard_map/ppermute | solution.py:411
  4.8 1.3 collective-permute-start.1
  6.1 0.8 slice.85
  6.9 0.8 slice.91
  7.7 0.0 collective-permute-done.xlo
  7.7 0.1 collective-permute-done.1.xhi
  7.9 0.8 fusion.11
  8.7 3.7 %collective-permute-start.2 = (f32[5,40,128]{2,1,0:T(8,128)S(1)}, f32[5,40,128]{2,1,0:T(8,128)S(1)}, u32[]{:S(2)}, u32[]{:S(2)}) collective-permute-start(f32[5,40,128]{2,1,0:T(8,128)S(1)} %pad_maximum_fusion), channel_id=1, source_target_pairs={{0,1},{1,2},{2,3},{3,4},{4,5},{5,6},{6,7},{7,8},{8,9},{9,10},{10,1... | collective-permute-start | bytes 307208 | tf_op jit(solution)/shard_map/ppermute | solution.py:411
  12.4 0.8 fusion.10
  13.3 0.1 collective-permute-start.3
  13.4 0.7 collective-permute-done.2.ylo
  14.1 3.6 %collective-permute-done.3.yhi = f32[5,40,128]{2,1,0:T(8,128)S(1)} collective-permute-done((f32[5,40,128]{2,1,0:T(8,128)S(1)}, f32[5,40,128]{2,1,0:T(8,128)S(1)}, u32[]{:S(2)}, u32[]{:S(2)}) %collective-permute-start.3) | collective-permute-done | bytes 102432 | tf_op jit(solution)/shard_map/ppermute | solution.py:411
  17.7 0.0 copy-start
  17.7 1.0 copy-done
  18.7 5.6 %step_one.1 = (f32[19,32,16,128]{3,2,1,0:T(8,128)S(1)}, f32[5,16,128]{2,1,0:T(8,128)S(1)}, f32[5,16,128]{2,1,0:T(8,128)S(1)}, f32[5,40,128]{2,1,0:T(8,128)S(1)}, f32[5,40,128]{2,1,0:T(8,128)S(1)}) custom-call(f32[19,32,16,128]{3,2,1,0:T(8,128)} %pops.3, f32[34,16,128]{2,1,0:T(8,128)S(1)} %copy-done, f32[5,16,128]{2,1,0:T(8,128)S(1)} %collective-permute-done.xlo, ...), custom_call_target="tpu_custom_call" | custom-call | tf_op jit(solution)/shard_map/step_one/pallas_call | solution.py:351
  24.3 1.3 collective-permute-start.4
  25.6 1.6 collective-permute-start.5
  27.1 1.3 collective-permute-done.4.xlo
  28.4 0.1 collective-permute-done.5.xhi
  28.5 0.1 fusion.9
  28.6 1.1 collective-permute-start.6
  29.7 0.1 fusion.8
  29.8 1.9 %collective-permute-start.7 = (f32[5,40,128]{2,1,0:T(8,128)S(1)}, f32[5,40,128]{2,1,0:T(8,128)S(1)}, u32[]{:S(2)}, u32[]{:S(2)}) collective-permute-start(f32[5,40,128]{2,1,0:T(8,128)S(1)} %pad_maximum_fusion.3), channel_id=1, source_target_pairs={{1,0},{2,1},{3,2},{4,3},{5,4},{6,5},{7,6},{8,7},{9,8},{10,9},{11,1... | collective-permute-start | bytes 307208 | tf_op jit(solution)/shard_map/ppermute | solution.py:411
  31.7 0.0 copy-done.1
  31.7 0.6 collective-permute-done.6.ylo
  32.3 1.7 collective-permute-done.7.yhi
  34.0 8.9 %step_two.1 = f32[32,616,128]{2,1,0:T(8,128)} custom-call(s32[16]{0:T(128)S(1)} %and_select_fusion.owners, f32[19,32,16,128]{3,2,1,0:T(8,128)S(1)} %get-tuple-element.20.f1, f32[5,16,128]{2,1,0:T(8,128)S(1)} %collective-permute-done.4.xlo, f32[5,16,128]{2,1,0:T(8,128)S(1)} %collective-permute-done.5.xhi, f32[5,40,128]{2,1,0:T(8,128)S(1)} %collective-permute-done.6.ylo, ...), custom_call_target="tpu_custom_call" | custom-call | tf_op jit(solution)/shard_map/step_two/pallas_call | solution.py:370
  42.9 125.8 %all_to_all.5.incoming = f32[32,616,128]{2,1,0:T(8,128)} all-to-all(f32[32,616,128]{2,1,0:T(8,128)} %step_two.1), channel_id=1, replica_groups=mesh['slab'=4,'blk'=32] {'blk'}, dimensions={0} | all-to-all | bytes 20185088 | tf_op jit(solution)/shard_map/all_to_all | solution.py:441
  168.7 5.9 %place.1 = f32[19,16,4096]{2,1,0:T(8,128)} custom-call(f32[32,616,128]{2,1,0:T(8,128)} %all_to_all.5.incoming), custom_call_target="tpu_custom_call" | custom-call | tf_op jit(solution)/shard_map/place/pallas_call | solution.py:390
  (12 shorter events, 0.1 us)
Async XLA Ops:
  2.7 29.0 %copy-start.1 = (s32[1,16]{1,0:T(1,128)S(1)}, s32[1,16]{1,0:T(1,128)}, u32[]{:S(2)}) copy-start(s32[1,16]{1,0:T(1,128)} %param.7) | copy-start | bytes 196
  2.7 5.0 %collective-permute-start = (f32[5,16,128]{2,1,0:T(8,128)}, f32[5,16,128]{2,1,0:T(8,128)S(1)}, u32[]{:S(2)}, u32[]{:S(2)}) collective-permute-start(f32[5,16,128]{2,1,0:T(8,128)} %get-tuple-element.16), channel_id=1, source_target_pairs={{0,32},{32,64},{64,96},{96,0},{1,33},{33,65},{65,97},{97,1},{2,34}... | collective-permute-start | bytes 122888 | tf_op jit(solution)/shard_map/ppermute | solution.py:411
  4.8 3.1 %collective-permute-start.1 = (f32[5,16,128]{2,1,0:T(8,128)}, f32[5,16,128]{2,1,0:T(8,128)S(1)}, u32[]{:S(2)}, u32[]{:S(2)}) collective-permute-start(f32[5,16,128]{2,1,0:T(8,128)} %get-tuple-element.17), channel_id=1, source_target_pairs={{32,0},{64,32},{96,64},{0,96},{33,1},{65,33},{97,65},{1,97},{34,2}... | collective-permute-start | bytes 122888 | tf_op jit(solution)/shard_map/ppermute | solution.py:411
  8.7 5.4 %collective-permute-start.2 = (f32[5,40,128]{2,1,0:T(8,128)S(1)}, f32[5,40,128]{2,1,0:T(8,128)S(1)}, u32[]{:S(2)}, u32[]{:S(2)}) collective-permute-start(f32[5,40,128]{2,1,0:T(8,128)S(1)} %pad_maximum_fusion), channel_id=1, source_target_pairs={{0,1},{1,2},{2,3},{3,4},{4,5},{5,6},{6,7},{7,8},{8,9},{9,10},{10,1... | collective-permute-start | bytes 307208 | tf_op jit(solution)/shard_map/ppermute | solution.py:411
  13.3 4.4 %collective-permute-start.3 = (f32[5,40,128]{2,1,0:T(8,128)S(1)}, f32[5,40,128]{2,1,0:T(8,128)S(1)}, u32[]{:S(2)}, u32[]{:S(2)}) collective-permute-start(f32[5,40,128]{2,1,0:T(8,128)S(1)} %pad_maximum_fusion.1), channel_id=1, source_target_pairs={{1,0},{2,1},{3,2},{4,3},{5,4},{6,5},{7,6},{8,7},{9,8},{10,9},{11,1... | collective-permute-start | bytes 307208 | tf_op jit(solution)/shard_map/ppermute | solution.py:411
  17.7 1.0 copy-start
  24.3 4.1 %collective-permute-start.4 = (f32[5,16,128]{2,1,0:T(8,128)S(1)}, f32[5,16,128]{2,1,0:T(8,128)S(1)}, u32[]{:S(2)}, u32[]{:S(2)}) collective-permute-start(f32[5,16,128]{2,1,0:T(8,128)S(1)} %get-tuple-element.21), channel_id=1, source_target_pairs={{0,32},{32,64},{64,96},{96,0},{1,33},{33,65},{65,97},{97,1},{2,34}... | collective-permute-start | bytes 122888 | tf_op jit(solution)/shard_map/ppermute | solution.py:411
  25.6 2.9 %collective-permute-start.5 = (f32[5,16,128]{2,1,0:T(8,128)S(1)}, f32[5,16,128]{2,1,0:T(8,128)S(1)}, u32[]{:S(2)}, u32[]{:S(2)}) collective-permute-start(f32[5,16,128]{2,1,0:T(8,128)S(1)} %get-tuple-element.22), channel_id=1, source_target_pairs={{32,0},{64,32},{96,64},{0,96},{33,1},{65,33},{97,65},{1,97},{34,2}... | collective-permute-start | bytes 122888 | tf_op jit(solution)/shard_map/ppermute | solution.py:411
  28.6 3.7 %collective-permute-start.6 = (f32[5,40,128]{2,1,0:T(8,128)S(1)}, f32[5,40,128]{2,1,0:T(8,128)S(1)}, u32[]{:S(2)}, u32[]{:S(2)}) collective-permute-start(f32[5,40,128]{2,1,0:T(8,128)S(1)} %pad_maximum_fusion.2), channel_id=1, source_target_pairs={{0,1},{1,2},{2,3},{3,4},{4,5},{5,6},{6,7},{7,8},{8,9},{9,10},{10,1... | collective-permute-start | bytes 307208 | tf_op jit(solution)/shard_map/ppermute | solution.py:411
  29.8 4.2 %collective-permute-start.7 = (f32[5,40,128]{2,1,0:T(8,128)S(1)}, f32[5,40,128]{2,1,0:T(8,128)S(1)}, u32[]{:S(2)}, u32[]{:S(2)}) collective-permute-start(f32[5,40,128]{2,1,0:T(8,128)S(1)} %pad_maximum_fusion.3), channel_id=1, source_target_pairs={{1,0},{2,1},{3,2},{4,3},{5,4},{6,5},{7,6},{8,7},{9,8},{10,9},{11,1... | collective-permute-start | bytes 307208 | tf_op jit(solution)/shard_map/ppermute | solution.py:411

commit v4 on v2

--- a/solution.py
+++ b/solution.py
@@ -124,7 +124,7 @@
     return y_row
 
 
-def prep_kernel(pops, solid, wetting, mark, xup, xdn, yup, ydn, x_planes, y_tiles, sem_x, sem_y):
+def prep_kernel(pops, mark, xup, xdn, yup, ydn, x_planes, y_tiles, sem_x, sem_y):
     copies = []
     for k in range(5):
         copies.append(pltpu.make_async_copy(pops.at[X_UP[k], XS - 1], x_planes.at[k], sem_x.at[k]))
@@ -133,19 +133,14 @@
         copies.append(pltpu.make_async_copy(pops.at[Y_DOWN[k], :, 0:8], y_tiles.at[5 + k], sem_y.at[5 + k]))
     for copy in copies:
         copy.start()
-    clear = jnp.zeros((YS, ZS), jnp.float32)
-    mark[0] = clear
-    mark[XS + 1] = clear
-    for x in range(XS):
-        mark[x + 1] = jnp.where(solid[x] == 1, jnp.where(wetting[x] == 1, -BIG, BIG), 0.0)
     for copy in copies:
         copy.wait()
     for k in range(5):
-        for out, at, x in ((xup, k, XS), (xdn, 5 + k, 1)):
+        for out, at, x in ((xup, k, XS - 1), (xdn, 5 + k, 0)):
             m = mark[x]
             out[k] = jnp.where(m == 0.0, x_planes[at], m)
     for out, first, y in ((yup, 0, 7), (ydn, 5, 0)):
-        m = mark[1 : XS + 1, y + (8 if first == 0 else 0), :]
+        m = mark[:, y + (8 if first == 0 else 0), :]
         for k in range(5):
             out[k, 1 : XS + 1, :] = jnp.where(m == 0.0, y_tiles[first + k, :, y, :], m)
 
@@ -156,7 +151,11 @@
         copy.start()
     place_x_halo(f, xlo, xhi)
     def plane(x, carry):
-        marked = {c: mark[x + 1 - c] for c in (-1, 0, 1)}
+        marked = {
+            0: mark[x],
+            1: jnp.where(x == 0, 0.0, mark[jnp.maximum(x - 1, 0)]),
+            -1: jnp.where(x == XS - 1, 0.0, mark[jnp.minimum(x + 1, XS - 1)]),
+        }
 
         def source(i):
             c = VELOCITIES[i][0]
@@ -179,7 +178,7 @@
     for c in range(CHUNKS):
         if c + 1 < CHUNKS:
             copies[c + 1].wait()
-        lax.fori_loop(c * CHUNK, (c + 1) * CHUNK, plane, 0)
+        lax.fori_loop(c * CHUNK, (c + 1) * CHUNK, plane, 0, unroll=2)
         at = pl.ds(c * CHUNK, CHUNK)
         outs.append(pltpu.make_async_copy(res.at[:, at], out.at[:, at], sem_out.at[c]))
         outs[-1].start()
@@ -220,13 +219,15 @@
         )
         fluid = jnp.abs(f[0, x + 1]) < HALF_BIG
         base = x // 16 * (8 * SLOT_ROWS) + x % 16 * 2
+        tiles = []
         for i in range(19):
             value = jnp.where(fluid, new[i], 0.0)
-            for half in range(2):
-                v = pltpu.roll(value[half * 8 : half * 8 + 8], 0, 1, stride=16, stride_axis=0)
-                v = jnp.take_along_axis(v, pick, axis=0)
-                v = pltpu.roll(v, 16, 1, stride=16, stride_axis=0)
-                buf[pl.ds(base + i * 32 + half, 8, stride=SLOT_ROWS + 1), :] = v
+            tiles += [(i * 32 + half, value[half * 8 : half * 8 + 8]) for half in range(2)]
+        tiles = [(at, pltpu.roll(v, 0, 1, stride=16, stride_axis=0)) for at, v in tiles]
+        tiles = [(at, jnp.take_along_axis(v, pick, axis=0)) for at, v in tiles]
+        tiles = [(at, pltpu.roll(v, 16, 1, stride=16, stride_axis=0)) for at, v in tiles]
+        for at, v in tiles:
+            buf[pl.ds(base + at, 8, stride=SLOT_ROWS), :] = v
         return carry
 
     outs = []
@@ -234,7 +235,7 @@
     for c in range(CHUNKS):
         if c + 1 < CHUNKS:
             copies[c + 1].wait()
-        lax.fori_loop(c * CHUNK, (c + 1) * CHUNK, plane, 0)
+        lax.fori_loop(c * CHUNK, (c + 1) * CHUNK, plane, 0, unroll=2)
         if c == 0:
             for clear in clears:
                 clear.wait()
@@ -277,9 +278,9 @@
 
         def channel(i, carry):
             for j in range(32):
-                at = h * 8 * SLOT_ROWS + 7 + i * 32 + j
+                at = h * 8 * SLOT_ROWS + i * 32 + j
                 res[i, h * 8 : h * 8 + 8, j * 128 : (j + 1) * 128] = blocks[
-                    pl.ds(at, 8, stride=SLOT_ROWS - 1), :
+                    pl.ds(at, 8, stride=SLOT_ROWS), :
                 ]
             return carry
 
@@ -301,28 +302,28 @@
     return jax.ShapeDtypeStruct(shape, jnp.float32)
 
 
-def params():
-    return pltpu.CompilerParams(vmem_limit_bytes=48 * 1024 * 1024)
+def params(mib=48):
+    return pltpu.CompilerParams(vmem_limit_bytes=mib * 1024 * 1024)
 
 
 EDGES = (sds(5, YS, ZS), sds(5, YS, ZS), sds(5, HALO_ROWS, ZS), sds(5, HALO_ROWS, ZS))
 
 
-def prep(pops, solid, wetting):
+def prep(pops, mark):
     return pl.pallas_call(
         prep_kernel,
-        out_shape=(sds(XS + 2, YS, ZS), *EDGES),
-        in_specs=[ANY, VMEM, VMEM],
-        out_specs=(VMEM,) * 5,
+        out_shape=EDGES,
+        in_specs=[ANY, VMEM],
+        out_specs=(VMEM,) * 4,
         scratch_shapes=[
             pltpu.VMEM((10, YS, ZS), jnp.float32),
             pltpu.VMEM((10, XS, 8, ZS), jnp.float32),
             pltpu.SemaphoreType.DMA((10,)),
             pltpu.SemaphoreType.DMA((10,)),
         ],
-        compiler_params=params(),
+        compiler_params=params(50),
         name="prep",
-    )(pops, solid, wetting)
+    )(pops, mark)
 
 
 def step_one(pops, mark, halo):
@@ -411,7 +412,8 @@
 
 def per_device(populations, solid, wetting, dest):
     peers = lax.axis_size("blk")
-    mark, *edges = prep(populations, solid, wetting)
+    mark = jnp.where(solid == 1, jnp.where(wetting == 1, -BIG, BIG), 0.0)
+    edges = prep(populations, mark)
     f1, *edges = step_one(populations, mark, exchange(*edges))
     outgoing = step_two(dest[0] // BLOCKS, f1, exchange(*edges), peers)
     incoming = lax.all_to_all(outgoing, "blk", split_axis=0, concat_axis=0, tiled=True)

time: 179 us -> 172 us (0.961)
  local copies, waits for them, and re-layouts: 4.33 us -> 0.02 us
  Pallas kernels: 25.2 us -> 21.8 us
    unnamed x8 -> x2, local copies, waits for them, and re-layouts: 4.32 us -> 0.01 us
    pallas_call x1, Pallas kernels: 12.5 us -> 8.93 us  [step_two(): pl.pallas_call(step_two_kernel, out_shape=sds(peers, SLOT_ROWS, ZS), in_s...]
where the time goes in v4:
time: 172 us
  blocking collectives  126 us (73%)
  Pallas kernels  21.8 us (13%)
  starting transfers between devices  13.1 us (8%)
  waiting for transfers between devices  9.45 us (5%)
    all_to_all x1, blocking collectives, per_device(): lax.all_to_all(outgoing, 'blk', split_axis=0, concat_axis=0, tiled=True)  126 us
    ppermute x8, starting transfers between devices, shift(): return lax.ppermute(value, axis, steps)  13.1 us
    ppermute x8, waiting for transfers between devices, shift(): return lax.ppermute(value, axis, steps)  9.45 us
    pallas_call x1, Pallas kernels, step_two(): pl.pallas_call(step_two_kernel, out_shape=sds(peers, SLOT_ROWS, ZS), in_s...  8.93 us
    pallas_call x1, Pallas kernels, step_one(): pl.pallas_call(step_one_kernel, out_shape=(sds(19, XS, YS, ZS), *EDGES),...  5.73 us
    pallas_call x1, Pallas kernels, place(): pl.pallas_call(place_kernel, out_shape=sds(19, BLOCKS, 4096), in_specs=[A...  5.31 us
  transfers between devices with their start and end apart: 8, of which 8 were waited for; matrix products, arithmetic and copies ran while one was open for 0% of the time, Pallas kernels for 0%

profile of v4, /device:TPU:1, one launch (start us, length us, event | category | flops | bytes accessed | tf_op | source)
XLA Modules:
  0.0 171.6 jit_solution(4040741124825481613)
XLA Ops:
  0.0 1.1 select_select_fusion.mark
  1.1 0.0 copy-start
  1.1 1.8 %prep.1 = (f32[5,16,128]{2,1,0:T(8,128)S(1)}, f32[5,16,128]{2,1,0:T(8,128)S(1)}, f32[5,40,128]{2,1,0:T(8,128)S(1)}, f32[5,40,128]{2,1,0:T(8,128)S(1)}) custom-call(f32[19,32,16,128]{3,2,1,0:T(8,128)} %pops.3, f32[32,16,128]{2,1,0:T(8,128)S(1)} %select_select_fusion.mark), custom_call_target="tpu_custom_call" | custom-call | tf_op jit(solution)/shard_map/prep/pallas_call | solution.py:313
  2.9 2.1 %collective-permute-start = (f32[5,16,128]{2,1,0:T(8,128)S(1)}, f32[5,16,128]{2,1,0:T(8,128)S(1)}, u32[]{:S(2)}, u32[]{:S(2)}) collective-permute-start(f32[5,16,128]{2,1,0:T(8,128)S(1)} %get-tuple-element.14), channel_id=1, source_target_pairs={{0,32},{32,64},{64,96},{96,0},{1,33},{33,65},{65,97},{97,1},{2,34}... | collective-permute-start | bytes 122888 | tf_op jit(solution)/shard_map/ppermute | solution.py:388
  5.0 1.3 collective-permute-start.1
  6.4 1.3 collective-permute-done.xlo
  7.7 0.2 collective-permute-done.1.xhi
  7.9 0.1 fusion.11
  8.0 3.7 %collective-permute-start.2 = (f32[5,40,128]{2,1,0:T(8,128)S(1)}, f32[5,40,128]{2,1,0:T(8,128)S(1)}, u32[]{:S(2)}, u32[]{:S(2)}) collective-permute-start(f32[5,40,128]{2,1,0:T(8,128)S(1)} %pad_maximum_fusion), channel_id=1, source_target_pairs={{0,1},{1,2},{2,3},{3,4},{4,5},{5,6},{6,7},{7,8},{8,9},{9,10},{10,1... | collective-permute-start | bytes 307208 | tf_op jit(solution)/shard_map/ppermute | solution.py:388
  11.7 0.1 fusion.10
  11.8 0.1 collective-permute-start.3
  11.8 1.5 collective-permute-done.2.ylo
  13.3 2.9 %collective-permute-done.3.yhi = f32[5,40,128]{2,1,0:T(8,128)S(1)} collective-permute-done((f32[5,40,128]{2,1,0:T(8,128)S(1)}, f32[5,40,128]{2,1,0:T(8,128)S(1)}, u32[]{:S(2)}, u32[]{:S(2)}) %collective-permute-start.3) | collective-permute-done | bytes 102432 | tf_op jit(solution)/shard_map/ppermute | solution.py:388
  16.2 5.7 %step_one.1 = (f32[19,32,16,128]{3,2,1,0:T(8,128)S(1)}, f32[5,16,128]{2,1,0:T(8,128)S(1)}, f32[5,16,128]{2,1,0:T(8,128)S(1)}, f32[5,40,128]{2,1,0:T(8,128)S(1)}, f32[5,40,128]{2,1,0:T(8,128)S(1)}) custom-call(f32[19,32,16,128]{3,2,1,0:T(8,128)} %pops.3, f32[32,16,128]{2,1,0:T(8,128)S(1)} %select_select_fusion.mark, ...), custom_call_target="tpu_custom_call" | custom-call | tf_op jit(solution)/shard_map/step_one/pallas_call | solution.py:330
  22.0 1.3 collective-permute-start.4
  23.2 1.6 collective-permute-start.5
  24.8 1.3 collective-permute-done.4.xlo
  26.1 0.1 collective-permute-done.5.xhi
  26.2 0.1 fusion.9
  26.3 1.1 collective-permute-start.6
  27.4 0.1 fusion.8
  27.5 1.9 %collective-permute-start.7 = (f32[5,40,128]{2,1,0:T(8,128)S(1)}, f32[5,40,128]{2,1,0:T(8,128)S(1)}, u32[]{:S(2)}, u32[]{:S(2)}) collective-permute-start(f32[5,40,128]{2,1,0:T(8,128)S(1)} %pad_maximum_fusion.3), channel_id=1, source_target_pairs={{1,0},{2,1},{3,2},{4,3},{5,4},{6,5},{7,6},{8,7},{9,8},{10,9},{11,1... | collective-permute-start | bytes 307208 | tf_op jit(solution)/shard_map/ppermute | solution.py:388
  29.4 0.0 copy-done
  29.4 0.6 collective-permute-done.6.ylo
  30.0 1.7 collective-permute-done.7.yhi
  31.6 8.9 %step_two.1 = f32[32,616,128]{2,1,0:T(8,128)} custom-call(s32[16]{0:T(128)S(1)} %and_select_fusion.owners, f32[19,32,16,128]{3,2,1,0:T(8,128)S(1)} %get-tuple-element.18.f1, f32[5,16,128]{2,1,0:T(8,128)S(1)} %collective-permute-done.4.xlo, f32[5,16,128]{2,1,0:T(8,128)S(1)} %collective-permute-done.5.xhi, f32[5,40,128]{2,1,0:T(8,128)S(1)} %collective-permute-done.6.ylo, ...), custom_call_target="tpu_custom_call" | custom-call | tf_op jit(solution)/shard_map/step_two/pallas_call | solution.py:347
  40.6 125.7 %all_to_all.5.incoming = f32[32,616,128]{2,1,0:T(8,128)} all-to-all(f32[32,616,128]{2,1,0:T(8,128)} %step_two.1), channel_id=1, replica_groups=mesh['slab'=4,'blk'=32] {'blk'}, dimensions={0} | all-to-all | bytes 20185088 | tf_op jit(solution)/shard_map/all_to_all | solution.py:419
  166.3 5.3 %place.1 = f32[19,16,4096]{2,1,0:T(8,128)} custom-call(f32[32,616,128]{2,1,0:T(8,128)} %all_to_all.5.incoming), custom_call_target="tpu_custom_call" | custom-call | tf_op jit(solution)/shard_map/place/pallas_call | solution.py:367
  (14 shorter events, 0.1 us)
Async XLA Ops:
  1.1 28.3 %copy-start = (s32[1,16]{1,0:T(1,128)S(1)}, s32[1,16]{1,0:T(1,128)}, u32[]{:S(2)}) copy-start(s32[1,16]{1,0:T(1,128)} %param.7) | copy-start | bytes 196
  2.9 4.8 %collective-permute-start = (f32[5,16,128]{2,1,0:T(8,128)S(1)}, f32[5,16,128]{2,1,0:T(8,128)S(1)}, u32[]{:S(2)}, u32[]{:S(2)}) collective-permute-start(f32[5,16,128]{2,1,0:T(8,128)S(1)} %get-tuple-element.14), channel_id=1, source_target_pairs={{0,32},{32,64},{64,96},{96,0},{1,33},{33,65},{65,97},{97,1},{2,34}... | collective-permute-start | bytes 122888 | tf_op jit(solution)/shard_map/ppermute | solution.py:388
  5.0 2.9 %collective-permute-start.1 = (f32[5,16,128]{2,1,0:T(8,128)S(1)}, f32[5,16,128]{2,1,0:T(8,128)S(1)}, u32[]{:S(2)}, u32[]{:S(2)}) collective-permute-start(f32[5,16,128]{2,1,0:T(8,128)S(1)} %get-tuple-element.15), channel_id=1, source_target_pairs={{32,0},{64,32},{96,64},{0,96},{33,1},{65,33},{97,65},{1,97},{34,2}... | collective-permute-start | bytes 122888 | tf_op jit(solution)/shard_map/ppermute | solution.py:388
  8.0 5.4 %collective-permute-start.2 = (f32[5,40,128]{2,1,0:T(8,128)S(1)}, f32[5,40,128]{2,1,0:T(8,128)S(1)}, u32[]{:S(2)}, u32[]{:S(2)}) collective-permute-start(f32[5,40,128]{2,1,0:T(8,128)S(1)} %pad_maximum_fusion), channel_id=1, source_target_pairs={{0,1},{1,2},{2,3},{3,4},{4,5},{5,6},{6,7},{7,8},{8,9},{9,10},{10,1... | collective-permute-start | bytes 307208 | tf_op jit(solution)/shard_map/ppermute | solution.py:388
  11.8 4.4 %collective-permute-start.3 = (f32[5,40,128]{2,1,0:T(8,128)S(1)}, f32[5,40,128]{2,1,0:T(8,128)S(1)}, u32[]{:S(2)}, u32[]{:S(2)}) collective-permute-start(f32[5,40,128]{2,1,0:T(8,128)S(1)} %pad_maximum_fusion.1), channel_id=1, source_target_pairs={{1,0},{2,1},{3,2},{4,3},{5,4},{6,5},{7,6},{8,7},{9,8},{10,9},{11,1... | collective-permute-start | bytes 307208 | tf_op jit(solution)/shard_map/ppermute | solution.py:388
  22.0 4.1 %collective-permute-start.4 = (f32[5,16,128]{2,1,0:T(8,128)S(1)}, f32[5,16,128]{2,1,0:T(8,128)S(1)}, u32[]{:S(2)}, u32[]{:S(2)}) collective-permute-start(f32[5,16,128]{2,1,0:T(8,128)S(1)} %get-tuple-element.19), channel_id=1, source_target_pairs={{0,32},{32,64},{64,96},{96,0},{1,33},{33,65},{65,97},{97,1},{2,34}... | collective-permute-start | bytes 122888 | tf_op jit(solution)/shard_map/ppermute | solution.py:388
  23.2 2.9 %collective-permute-start.5 = (f32[5,16,128]{2,1,0:T(8,128)S(1)}, f32[5,16,128]{2,1,0:T(8,128)S(1)}, u32[]{:S(2)}, u32[]{:S(2)}) collective-permute-start(f32[5,16,128]{2,1,0:T(8,128)S(1)} %get-tuple-element.20), channel_id=1, source_target_pairs={{32,0},{64,32},{96,64},{0,96},{33,1},{65,33},{97,65},{1,97},{34,2}... | collective-permute-start | bytes 122888 | tf_op jit(solution)/shard_map/ppermute | solution.py:388
  26.3 3.7 %collective-permute-start.6 = (f32[5,40,128]{2,1,0:T(8,128)S(1)}, f32[5,40,128]{2,1,0:T(8,128)S(1)}, u32[]{:S(2)}, u32[]{:S(2)}) collective-permute-start(f32[5,40,128]{2,1,0:T(8,128)S(1)} %pad_maximum_fusion.2), channel_id=1, source_target_pairs={{0,1},{1,2},{2,3},{3,4},{4,5},{5,6},{6,7},{7,8},{8,9},{9,10},{10,1... | collective-permute-start | bytes 307208 | tf_op jit(solution)/shard_map/ppermute | solution.py:388
  27.5 4.2 %collective-permute-start.7 = (f32[5,40,128]{2,1,0:T(8,128)S(1)}, f32[5,40,128]{2,1,0:T(8,128)S(1)}, u32[]{:S(2)}, u32[]{:S(2)}) collective-permute-start(f32[5,40,128]{2,1,0:T(8,128)S(1)} %pad_maximum_fusion.3), channel_id=1, source_target_pairs={{1,0},{2,1},{3,2},{4,3},{5,4},{6,5},{7,6},{8,7},{9,8},{10,9},{11,1... | collective-permute-start | bytes 307208 | tf_op jit(solution)/shard_map/ppermute | solution.py:388

commit v5 on v4

--- a/solution.py
+++ b/solution.py
@@ -31,6 +31,7 @@
 BLOCKS = 16
 BLOCK_ROWS = 19 * 32
 SLOT_ROWS = BLOCK_ROWS + 8
+CHUNK_ROWS = 19 * 2 * CHUNK
 
 
 def collide(f):
@@ -89,8 +90,8 @@
         if cz:
             v = pltpu.roll(v, cz % ZS, 1)
         reflected = mine[OPPOSITE[i]]
-        wall = jnp.where(v > 0.0, reflected, 2.0 * WALL_DENSITY * WEIGHTS[i] - reflected)
-        out.append(jnp.where(jnp.abs(v) < HALF_BIG, v, wall))
+        v = jnp.where(v < HALF_BIG, v, reflected)
+        out.append(jnp.where(v > -HALF_BIG, v, 2.0 * WALL_DENSITY * WEIGHTS[i] - reflected))
     return out
 
 
@@ -111,41 +112,52 @@
         f[X_DOWN[k], XS + 1] = jnp.where(last, BIG, xhi[k])
 
 
-def y_rows(ylo, yhi, x):
+def y_rows(inner, outer, x):
     first = lax.axis_index("blk") == 0
     last = lax.axis_index("blk") == lax.axis_size("blk") - 1
+    even = lax.axis_index("blk") % 2 == 0
 
     def y_row(i):
         at = x + 1 - VELOCITIES[i][0]
+        k = Y_UP.index(i) if i in Y_UP else Y_DOWN.index(i)
+        a, b = inner[k, pl.ds(at, 1), :], outer[k, pl.ds(at, 1), :]
         if i in Y_UP:
-            return jnp.where(first, BIG, ylo[Y_UP.index(i), pl.ds(at, 1), :])
-        return jnp.where(last, BIG, yhi[Y_DOWN.index(i), pl.ds(at, 1), :])
+            return jnp.where(first, BIG, jnp.where(even, b, a))
+        return jnp.where(last, BIG, jnp.where(even, a, b))
 
     return y_row
 
 
-def prep_kernel(pops, mark, xup, xdn, yup, ydn, x_planes, y_tiles, sem_x, sem_y):
+def x_edges_kernel(pops, mark, xup, xdn, planes, sem):
     copies = []
     for k in range(5):
-        copies.append(pltpu.make_async_copy(pops.at[X_UP[k], XS - 1], x_planes.at[k], sem_x.at[k]))
-        copies.append(pltpu.make_async_copy(pops.at[X_DOWN[k], 0], x_planes.at[5 + k], sem_x.at[5 + k]))
-        copies.append(pltpu.make_async_copy(pops.at[Y_UP[k], :, 8:16], y_tiles.at[k], sem_y.at[k]))
-        copies.append(pltpu.make_async_copy(pops.at[Y_DOWN[k], :, 0:8], y_tiles.at[5 + k], sem_y.at[5 + k]))
+        copies.append(pltpu.make_async_copy(pops.at[X_UP[k], XS - 1], planes.at[k], sem.at[k]))
+        copies.append(pltpu.make_async_copy(pops.at[X_DOWN[k], 0], planes.at[5 + k], sem.at[5 + k]))
     for copy in copies:
         copy.start()
     for copy in copies:
         copy.wait()
     for k in range(5):
-        for out, at, x in ((xup, k, XS - 1), (xdn, 5 + k, 0)):
-            m = mark[x]
-            out[k] = jnp.where(m == 0.0, x_planes[at], m)
+        for out, at, m in ((xup, k, mark[1]), (xdn, 5 + k, mark[0])):
+            out[k] = jnp.where(m == 0.0, planes[at], m)
+
+
+def y_edges_kernel(pops, mark, yup, ydn, tiles, sem):
+    copies = []
+    for k in range(5):
+        copies.append(pltpu.make_async_copy(pops.at[Y_UP[k], :, 8:16], tiles.at[k], sem.at[k]))
+        copies.append(pltpu.make_async_copy(pops.at[Y_DOWN[k], :, 0:8], tiles.at[5 + k], sem.at[5 + k]))
+    for copy in copies:
+        copy.start()
+    for copy in copies:
+        copy.wait()
     for out, first, y in ((yup, 0, 7), (ydn, 5, 0)):
         m = mark[:, y + (8 if first == 0 else 0), :]
         for k in range(5):
-            out[k, 1 : XS + 1, :] = jnp.where(m == 0.0, y_tiles[first + k, :, y, :], m)
-
-
-def step_one_kernel(pops, mark, xlo, xhi, ylo, yhi, out, xup, xdn, yup, ydn, f, res, sem_in, sem_out):
+            out[k, 1 : XS + 1, :] = jnp.where(m == 0.0, tiles[first + k, :, y, :], m)
+
+
+def step_one_kernel(pops, mark, xlo, xhi, inner, outer, out, xup, xdn, yup, ydn, f, sem_in):
     copies = fetch(pops, f, sem_in)
     for copy in copies:
         copy.start()
@@ -161,38 +173,29 @@
             c = VELOCITIES[i][0]
             return jnp.where(marked[c] == 0.0, f[i, x + 1 - c], marked[c])
 
-        pulled = pull(lambda i: f[i, x + 1], source, y_rows(ylo, yhi, x))
+        pulled = pull(lambda i: f[i, x + 1], source, y_rows(inner, outer, x))
         new = collide(pulled)
         here = marked[0]
         for i in range(19):
             value = jnp.where(here == 0.0, new[i], here)
-            res[i, x] = value
+            out[i, x] = value
             if i in Y_UP:
                 yup[Y_UP.index(i), pl.ds(x + 1, 1), :] = value[YS - 1 : YS]
             if i in Y_DOWN:
                 ydn[Y_DOWN.index(i), pl.ds(x + 1, 1), :] = value[0:1]
         return carry
 
-    outs = []
     copies[0].wait()
     for c in range(CHUNKS):
         if c + 1 < CHUNKS:
             copies[c + 1].wait()
         lax.fori_loop(c * CHUNK, (c + 1) * CHUNK, plane, 0, unroll=2)
-        at = pl.ds(c * CHUNK, CHUNK)
-        outs.append(pltpu.make_async_copy(res.at[:, at], out.at[:, at], sem_out.at[c]))
-        outs[-1].start()
     for k in range(5):
-        xup[k] = res[X_UP[k], XS - 1]
-        xdn[k] = res[X_DOWN[k], 0]
-    for copy in outs:
-        copy.wait()
-
-
-def step_two_kernel(owners, f1, xlo, xhi, ylo, yhi, outgoing, f, buf, absent, sem_in, sem_absent, sem_out):
-    copies = fetch(f1, f, sem_in)
-    for copy in copies:
-        copy.start()
+        xup[k] = out[X_UP[k], XS - 1]
+        xdn[k] = out[X_DOWN[k], 0]
+
+
+def step_two_kernel(owners, f, xlo, xhi, inner, outer, outgoing, buf, absent, sem_absent, sem_out):
     absent[...] = jnp.full((8, ZS), -1.0, jnp.float32)
     label_rows = pl.ds(BLOCK_ROWS, 8)
     clears = [
@@ -204,25 +207,28 @@
     for k in range(BLOCKS):
         at = (k // 8 * 8 + 7 - k % 8) * SLOT_ROWS + BLOCK_ROWS
         buf[at : at + 8, :] = jnp.full((8, ZS), float(k), jnp.float32)
-    place_x_halo(f, xlo, xhi)
+    first = lax.axis_index("slab") == 0
+    last = lax.axis_index("slab") == lax.axis_size("slab") - 1
     sub = lax.broadcasted_iota(jnp.int32, (8, ZS), 0)
     lane_block = lax.broadcasted_iota(jnp.int32, (8, ZS), 1) // 16
     pick = (lane_block + sub + 1) & 7
 
     def plane(x, carry):
-        new = collide(
-            pull(
-                lambda i: f[i, x + 1],
-                lambda i: f[i, x + 1 - VELOCITIES[i][0]],
-                y_rows(ylo, yhi, x),
-            )
-        )
-        fluid = jnp.abs(f[0, x + 1]) < HALF_BIG
-        base = x // 16 * (8 * SLOT_ROWS) + x % 16 * 2
+        def source(i):
+            at = x - VELOCITIES[i][0]
+            if isinstance(at, int) and at < 0:
+                return jnp.where(first, BIG, xlo[X_UP.index(i)])
+            if isinstance(at, int) and at == XS:
+                return jnp.where(last, BIG, xhi[X_DOWN.index(i)])
+            return f[i, at]
+
+        new = collide(pull(lambda i: f[i, x], source, y_rows(inner, outer, x)))
+        fluid = jnp.abs(f[0, x]) < HALF_BIG
+        base = x // 16 * (8 * SLOT_ROWS) + x % 16 // CHUNK * CHUNK_ROWS + x % CHUNK * 2
         tiles = []
         for i in range(19):
             value = jnp.where(fluid, new[i], 0.0)
-            tiles += [(i * 32 + half, value[half * 8 : half * 8 + 8]) for half in range(2)]
+            tiles += [(i * 2 * CHUNK + half, value[half * 8 : half * 8 + 8]) for half in range(2)]
         tiles = [(at, pltpu.roll(v, 0, 1, stride=16, stride_axis=0)) for at, v in tiles]
         tiles = [(at, jnp.take_along_axis(v, pick, axis=0)) for at, v in tiles]
         tiles = [(at, pltpu.roll(v, 16, 1, stride=16, stride_axis=0)) for at, v in tiles]
@@ -231,23 +237,27 @@
         return carry
 
     outs = []
-    copies[0].wait()
     for c in range(CHUNKS):
-        if c + 1 < CHUNKS:
-            copies[c + 1].wait()
-        lax.fori_loop(c * CHUNK, (c + 1) * CHUNK, plane, 0, unroll=2)
+        if c in (0, CHUNKS - 1):
+            for x in range(c * CHUNK, (c + 1) * CHUNK):
+                plane(x, 0)
+        else:
+            lax.fori_loop(c * CHUNK, (c + 1) * CHUNK, plane, 0, unroll=2)
         if c == 0:
             for clear in clears:
                 clear.wait()
-        if c % 4 == 3:
-            for k in range(c // 4 * 8, c // 4 * 8 + 8):
-                at = (k // 8 * 8 + 7 - k % 8) * SLOT_ROWS
-                outs.append(
-                    pltpu.make_async_copy(
-                        buf.at[pl.ds(at, SLOT_ROWS)], outgoing.at[owners[k]], sem_out.at[k]
-                    )
+        part = c % 4
+        rows = CHUNK_ROWS if part < 3 else CHUNK_ROWS + 8
+        for k in range(c // 4 * 8, c // 4 * 8 + 8):
+            at = (k // 8 * 8 + 7 - k % 8) * SLOT_ROWS + part * CHUNK_ROWS
+            outs.append(
+                pltpu.make_async_copy(
+                    buf.at[pl.ds(at, rows)],
+                    outgoing.at[owners[k], pl.ds(part * CHUNK_ROWS, rows)],
+                    sem_out.at[k * 4 + part],
                 )
-                outs[-1].start()
+            )
+            outs[-1].start()
     for copy in outs:
         copy.wait()
 
@@ -278,7 +288,7 @@
 
         def channel(i, carry):
             for j in range(32):
-                at = h * 8 * SLOT_ROWS + i * 32 + j
+                at = h * 8 * SLOT_ROWS + j // 8 * CHUNK_ROWS + i * 8 + j % 8
                 res[i, h * 8 : h * 8 + 8, j * 128 : (j + 1) * 128] = blocks[
                     pl.ds(at, 8, stride=SLOT_ROWS), :
                 ]
@@ -309,20 +319,16 @@
 EDGES = (sds(5, YS, ZS), sds(5, YS, ZS), sds(5, HALO_ROWS, ZS), sds(5, HALO_ROWS, ZS))
 
 
-def prep(pops, mark):
+def edges(kernel, name, edge, scratch, pops, mark):
     return pl.pallas_call(
-        prep_kernel,
-        out_shape=EDGES,
+        kernel,
+        out_shape=(edge, edge),
         in_specs=[ANY, VMEM],
-        out_specs=(VMEM,) * 4,
-        scratch_shapes=[
-            pltpu.VMEM((10, YS, ZS), jnp.float32),
-            pltpu.VMEM((10, XS, 8, ZS), jnp.float32),
-            pltpu.SemaphoreType.DMA((10,)),
-            pltpu.SemaphoreType.DMA((10,)),
-        ],
+        out_specs=(VMEM, VMEM),
+        scratch_shapes=[pltpu.VMEM(scratch, jnp.float32), pltpu.SemaphoreType.DMA((10,))],
         compiler_params=params(50),
-        name="prep",
+        cost_estimate=pl.CostEstimate(flops=10**6, bytes_accessed=3 * 10**6, transcendentals=0),
+        name=name,
     )(pops, mark)
 
 
@@ -331,11 +337,9 @@
         step_one_kernel,
         out_shape=(sds(19, XS, YS, ZS), *EDGES),
         in_specs=[ANY] + [VMEM] * 5,
-        out_specs=(ANY, VMEM, VMEM, VMEM, VMEM),
+        out_specs=(VMEM,) * 5,
         scratch_shapes=[
             pltpu.VMEM((19, XS + 2, YS, ZS), jnp.float32),
-            pltpu.VMEM((19, XS, YS, ZS), jnp.float32),
-            pltpu.SemaphoreType.DMA((CHUNKS,)),
             pltpu.SemaphoreType.DMA((CHUNKS,)),
         ],
         compiler_params=params(),
@@ -347,15 +351,13 @@
     return pl.pallas_call(
         step_two_kernel,
         out_shape=sds(peers, SLOT_ROWS, ZS),
-        in_specs=[SMEM, ANY] + [VMEM] * 4,
+        in_specs=[SMEM] + [VMEM] * 5,
         out_specs=ANY,
         scratch_shapes=[
-            pltpu.VMEM((19, XS + 2, YS, ZS), jnp.float32),
             pltpu.VMEM((BLOCKS * SLOT_ROWS, ZS), jnp.float32),
             pltpu.VMEM((8, ZS), jnp.float32),
-            pltpu.SemaphoreType.DMA((CHUNKS,)),
             pltpu.SemaphoreType.DMA((peers,)),
-            pltpu.SemaphoreType.DMA((BLOCKS,)),
+            pltpu.SemaphoreType.DMA((BLOCKS * 4,)),
         ],
         compiler_params=params(),
         name="step_two",
@@ -388,8 +390,8 @@
     return lax.ppermute(value, axis, steps)
 
 
-def exchange(xup, xdn, yup, ydn):
-    xlo, xhi = shift(xup, "slab", True), shift(xdn, "slab", False)
+def exchange(x_planes, yup, ydn):
+    xlo, xhi = x_planes
     first = lax.axis_index("slab") == 0
     last = lax.axis_index("slab") == lax.axis_size("slab") - 1
     row = jnp.arange(HALO_ROWS)[:, None]
@@ -407,15 +409,35 @@
 
     yup = corners(yup, 7, 10, YS - 1, Y_UP)
     ydn = corners(ydn, 9, 8, 0, Y_DOWN)
-    return xlo, xhi, shift(yup, "blk", True), shift(ydn, "blk", False)
+    even = lax.axis_index("blk") % 2 == 0
+    count = lax.axis_size("blk")
+    across = [((i + 1) ^ 1) - 1 for i in range(count)]
+    across = [(i, j if 0 <= j < count else i) for i, j in enumerate(across)]
+    outer = lax.ppermute(jnp.where(even, ydn, yup), "blk", across)
+    inner = lax.ppermute(jnp.where(even, yup, ydn), "blk", [(i, i ^ 1) for i in range(count)])
+    return xlo, xhi, inner, outer
 
 
 def per_device(populations, solid, wetting, dest):
     peers = lax.axis_size("blk")
-    mark = jnp.where(solid == 1, jnp.where(wetting == 1, -BIG, BIG), 0.0)
-    edges = prep(populations, mark)
-    f1, *edges = step_one(populations, mark, exchange(*edges))
-    outgoing = step_two(dest[0] // BLOCKS, f1, exchange(*edges), peers)
+
+    def marks(solid, wetting):
+        return jnp.where(solid == 1, jnp.where(wetting == 1, -BIG, BIG), 0.0)
+
+    def ends(kinds):
+        return jnp.stack([kinds[0], kinds[XS - 1]])
+
+    def x_exchange(xup, xdn):
+        return shift(xup, "slab", True), shift(xdn, "slab", False)
+
+    x_marks = marks(ends(solid), ends(wetting))
+    x_planes = x_exchange(
+        *edges(x_edges_kernel, "x_edges", sds(5, YS, ZS), (10, YS, ZS), populations, x_marks)
+    )
+    mark = marks(solid, wetting)
+    rows = edges(y_edges_kernel, "y_edges", sds(5, HALO_ROWS, ZS), (10, XS, 8, ZS), populations, mark)
+    f1, xup, xdn, yup, ydn = step_one(populations, mark, exchange(x_planes, *rows))
+    outgoing = step_two(dest[0] // BLOCKS, f1, exchange(x_exchange(xup, xdn), yup, ydn), peers)
     incoming = lax.all_to_all(outgoing, "blk", split_axis=0, concat_axis=0, tiled=True)
     return place(incoming).transpose(1, 0, 2)
 

time: 172 us -> 171 us (level)
  starting transfers between devices: 13.1 us -> 16.2 us
  waiting for transfers between devices: 9.45 us -> 6.44 us
  blocking collectives: 126 us -> 124 us
    ppermute x0 -> x4, starting transfers between devices: none -> 9.86 us  [the longest x2 9.69 us: exchange(): outer = lax.ppermute(jnp.where(even, ydn, yup), 'blk', across)]
    ppermute x8 -> x4, waiting for transfers between devices: 9.45 us -> 1.98 us  [shift(): return lax.ppermute(value, axis, steps)]
    ppermute x8 -> x4, starting transfers between devices: 13.1 us -> 6.3 us  [shift(): return lax.ppermute(value, axis, steps)]
    ppermute x0 -> x4, waiting for transfers between devices: none -> 4.45 us  [the longest x2 4.45 us: exchange(): outer = lax.ppermute(jnp.where(even, ydn, yup), 'blk', across)]
  transfers between devices with their start and end apart: 8 -> 8, of which waited for: 8 -> 4; matrix products, arithmetic and copies ran while one was open for 0% -> 0% of each run, Pallas kernels for 0% -> 1%
where the time goes in v5:
time: 171 us; the launch traced here: 170 us
  blocking collectives  124 us (73%)
  Pallas kernels  21.9 us (13%)
  starting transfers between devices  16.2 us (9%)
  waiting for transfers between devices  6.44 us (4%)
    all_to_all x1, blocking collectives, per_device(): lax.all_to_all(outgoing, 'blk', split_axis=0, concat_axis=0, tiled=True)  124 us
    ppermute x2, starting transfers between devices, exchange(): outer = lax.ppermute(jnp.where(even, ydn, yup), 'blk', across)  9.69 us
    pallas_call x1, Pallas kernels, step_two(): pl.pallas_call(step_two_kernel, out_shape=sds(peers, SLOT_ROWS, ZS), in_s...  8.9 us
    ppermute x4, starting transfers between devices, shift(): return lax.ppermute(value, axis, steps)  6.3 us
    pallas_call x1, Pallas kernels, place(): pl.pallas_call(place_kernel, out_shape=sds(19, BLOCKS, 4096), in_specs=[A...  5.31 us
    pallas_call x1, Pallas kernels, step_one(): pl.pallas_call(step_one_kernel, out_shape=(sds(19, XS, YS, ZS), *EDGES),...  5.19 us
    ppermute x2, waiting for transfers between devices, exchange(): outer = lax.ppermute(jnp.where(even, ydn, yup), 'blk', across)  4.45 us
  transfers between devices with their start and end apart: 8, of which 4 were waited for; matrix products, arithmetic and copies ran while one was open for 0% of the time, Pallas kernels for 1%

profile of v5, /device:TPU:1, one launch (start us, length us, event | category | flops | bytes accessed | tf_op | source)
XLA Modules:
  0.0 170.4 jit_solution(14017283871703953569)
XLA Ops:
  0.0 0.0 copy-start
  0.0 0.8 fusion.12
  0.8 0.9 x_edges.1
  1.8 2.1 %collective-permute-start = (f32[5,16,128]{2,1,0:T(8,128)S(1)}, f32[5,16,128]{2,1,0:T(8,128)S(1)}, u32[]{:S(2)}, u32[]{:S(2)}) collective-permute-start(f32[5,16,128]{2,1,0:T(8,128)S(1)} %get-tuple-element.14), channel_id=1, source_target_pairs={{0,32},{32,64},{64,96},{96,0},{1,33},{33,65},{65,97},{97,1},{2,34}... | collective-permute-start | bytes 122888 | tf_op jit(solution)/shard_map/ppermute | solution.py:390
  3.9 1.3 collective-permute-start.1
  5.2 0.0 copy-done
  5.2 0.0 copy-done.1
  5.3 0.0 copy-start.2
  5.3 1.6 y_edges.1
  7.0 0.0 collective-permute-done.xlo
  7.0 0.0 collective-permute-done.1.xhi
  7.0 0.1 fusion.16
  7.1 0.1 fusion.17
  7.2 5.2 %collective-permute-start.3 = (f32[5,40,128]{2,1,0:T(8,128)S(1)}, f32[5,40,128]{2,1,0:T(8,128)S(1)}, u32[]{:S(2)}, u32[]{:S(2)}) collective-permute-start(f32[5,40,128]{2,1,0:T(8,128)S(1)} %get-tuple-element.29), channel_id=1, source_target_pairs={{0,0},{1,2},{2,1},{3,4},{4,3},{5,6},{6,5},{7,8},{8,7},{9,10},{10,9... | collective-permute-start | bytes 307208 | tf_op jit(solution)/shard_map/ppermute | solution.py:416
  12.5 0.1 collective-permute-start.2
  12.6 2.2 %collective-permute-done.3.outer = f32[5,40,128]{2,1,0:T(8,128)S(1)} collective-permute-done((f32[5,40,128]{2,1,0:T(8,128)S(1)}, f32[5,40,128]{2,1,0:T(8,128)S(1)}, u32[]{:S(2)}, u32[]{:S(2)}) %collective-permute-start.3) | collective-permute-done | bytes 102432 | tf_op jit(solution)/shard_map/ppermute | solution.py:416
  14.8 0.0 collective-permute-done.2.inner
  14.8 5.2 %step_one.1 = (f32[19,32,16,128]{3,2,1,0:T(8,128)S(1)}, f32[5,16,128]{2,1,0:T(8,128)S(1)}, f32[5,16,128]{2,1,0:T(8,128)S(1)}, f32[5,40,128]{2,1,0:T(8,128)S(1)}, f32[5,40,128]{2,1,0:T(8,128)S(1)}) custom-call(f32[19,32,16,128]{3,2,1,0:T(8,128)} %pops.5, f32[32,16,128]{2,1,0:T(8,128)S(1)} %select_select_fusion.mark, ...), custom_call_target="tpu_custom_call" | custom-call | tf_op jit(solution)/shard_map/step_one/pallas_call | solution.py:336
  20.0 1.3 collective-permute-start.4
  21.3 1.6 collective-permute-start.5
  22.9 1.4 collective-permute-done.4.xlo
  24.2 0.6 collective-permute-done.5.xhi
  24.8 0.1 fusion.15
  24.9 0.1 fusion.14
  25.0 4.4 %collective-permute-start.7 = (f32[5,40,128]{2,1,0:T(8,128)S(1)}, f32[5,40,128]{2,1,0:T(8,128)S(1)}, u32[]{:S(2)}, u32[]{:S(2)}) collective-permute-start(f32[5,40,128]{2,1,0:T(8,128)S(1)} %get-tuple-element.27), channel_id=1, source_target_pairs={{0,0},{1,2},{2,1},{3,4},{4,3},{5,6},{6,5},{7,8},{8,7},{9,10},{10,9... | collective-permute-start | bytes 307208 | tf_op jit(solution)/shard_map/ppermute | solution.py:416
  29.5 0.1 collective-permute-start.6
  29.6 0.0 copy-done.2
  29.6 2.2 %collective-permute-done.7.outer = f32[5,40,128]{2,1,0:T(8,128)S(1)} collective-permute-done((f32[5,40,128]{2,1,0:T(8,128)S(1)}, f32[5,40,128]{2,1,0:T(8,128)S(1)}, u32[]{:S(2)}, u32[]{:S(2)}) %collective-permute-start.7) | collective-permute-done | bytes 102432 | tf_op jit(solution)/shard_map/ppermute | solution.py:416
  31.8 0.0 collective-permute-done.6.inner
  31.8 8.9 %step_two.1 = f32[32,616,128]{2,1,0:T(8,128)} custom-call(s32[16]{0:T(128)S(1)} %and_select_fusion.owners, f32[19,32,16,128]{3,2,1,0:T(8,128)S(1)} %get-tuple-element.18.f, f32[5,16,128]{2,1,0:T(8,128)S(1)} %collective-permute-done.4.xlo, f32[5,16,128]{2,1,0:T(8,128)S(1)} %collective-permute-done.5.xhi, f32[5,40,128]{2,1,0:T(8,128)S(1)} %collective-permute-done.6.inner, ...), custom_call_target="tpu_custom_call" | custom-call | tf_op jit(solution)/shard_map/step_two/pallas_call | solution.py:351
  40.7 124.3 %all_to_all.5.incoming = f32[32,616,128]{2,1,0:T(8,128)} all-to-all(f32[32,616,128]{2,1,0:T(8,128)} %step_two.1), channel_id=1, replica_groups=mesh['slab'=4,'blk'=32] {'blk'}, dimensions={0} | all-to-all | bytes 20185088 | tf_op jit(solution)/shard_map/all_to_all | solution.py:441
  165.1 5.3 %place.1 = f32[19,16,4096]{2,1,0:T(8,128)} custom-call(f32[32,616,128]{2,1,0:T(8,128)} %all_to_all.5.incoming), custom_call_target="tpu_custom_call" | custom-call | tf_op jit(solution)/shard_map/place/pallas_call | solution.py:369
  (15 shorter events, 0.2 us)
Async XLA Ops:
  0.0 5.2 %copy-start = (s32[32,16,128]{2,1,0:T(8,128)S(1)}, s32[32,16,128]{2,1,0:T(8,128)}, u32[]{:S(2)}) copy-start(s32[32,16,128]{2,1,0:T(8,128)} %param.6) | copy-start | bytes 786436
  0.0 5.2 %copy-start.1 = (s32[32,16,128]{2,1,0:T(8,128)S(1)}, s32[32,16,128]{2,1,0:T(8,128)}, u32[]{:S(2)}) copy-start(s32[32,16,128]{2,1,0:T(8,128)} %param.5) | copy-start | bytes 786436
  1.8 5.2 %collective-permute-start = (f32[5,16,128]{2,1,0:T(8,128)S(1)}, f32[5,16,128]{2,1,0:T(8,128)S(1)}, u32[]{:S(2)}, u32[]{:S(2)}) collective-permute-start(f32[5,16,128]{2,1,0:T(8,128)S(1)} %get-tuple-element.14), channel_id=1, source_target_pairs={{0,32},{32,64},{64,96},{96,0},{1,33},{33,65},{65,97},{97,1},{2,34}... | collective-permute-start | bytes 122888 | tf_op jit(solution)/shard_map/ppermute | solution.py:390
  3.9 3.1 %collective-permute-start.1 = (f32[5,16,128]{2,1,0:T(8,128)S(1)}, f32[5,16,128]{2,1,0:T(8,128)S(1)}, u32[]{:S(2)}, u32[]{:S(2)}) collective-permute-start(f32[5,16,128]{2,1,0:T(8,128)S(1)} %get-tuple-element.15), channel_id=1, source_target_pairs={{32,0},{64,32},{96,64},{0,96},{33,1},{65,33},{97,65},{1,97},{34,2}... | collective-permute-start | bytes 122888 | tf_op jit(solution)/shard_map/ppermute | solution.py:390
  5.3 24.3 %copy-start.2 = (s32[1,16]{1,0:T(1,128)S(1)}, s32[1,16]{1,0:T(1,128)}, u32[]{:S(2)}) copy-start(s32[1,16]{1,0:T(1,128)} %param.7) | copy-start | bytes 196
  7.2 7.6 %collective-permute-start.3 = (f32[5,40,128]{2,1,0:T(8,128)S(1)}, f32[5,40,128]{2,1,0:T(8,128)S(1)}, u32[]{:S(2)}, u32[]{:S(2)}) collective-permute-start(f32[5,40,128]{2,1,0:T(8,128)S(1)} %get-tuple-element.29), channel_id=1, source_target_pairs={{0,0},{1,2},{2,1},{3,4},{4,3},{5,6},{6,5},{7,8},{8,7},{9,10},{10,9... | collective-permute-start | bytes 307208 | tf_op jit(solution)/shard_map/ppermute | solution.py:416
  12.5 2.3 %collective-permute-start.2 = (f32[5,40,128]{2,1,0:T(8,128)S(1)}, f32[5,40,128]{2,1,0:T(8,128)S(1)}, u32[]{:S(2)}, u32[]{:S(2)}) collective-permute-start(f32[5,40,128]{2,1,0:T(8,128)S(1)} %get-tuple-element.30), channel_id=1, source_target_pairs={{0,1},{1,0},{2,3},{3,2},{4,5},{5,4},{6,7},{7,6},{8,9},{9,8},{10,11... | collective-permute-start | bytes 307208 | tf_op jit(solution)/shard_map/ppermute | solution.py:417
  20.0 4.2 %collective-permute-start.4 = (f32[5,16,128]{2,1,0:T(8,128)S(1)}, f32[5,16,128]{2,1,0:T(8,128)S(1)}, u32[]{:S(2)}, u32[]{:S(2)}) collective-permute-start(f32[5,16,128]{2,1,0:T(8,128)S(1)} %get-tuple-element.19), channel_id=1, source_target_pairs={{0,32},{32,64},{64,96},{96,0},{1,33},{33,65},{65,97},{97,1},{2,34}... | collective-permute-start | bytes 122888 | tf_op jit(solution)/shard_map/ppermute | solution.py:390
  21.3 3.5 %collective-permute-start.5 = (f32[5,16,128]{2,1,0:T(8,128)S(1)}, f32[5,16,128]{2,1,0:T(8,128)S(1)}, u32[]{:S(2)}, u32[]{:S(2)}) collective-permute-start(f32[5,16,128]{2,1,0:T(8,128)S(1)} %get-tuple-element.20), channel_id=1, source_target_pairs={{32,0},{64,32},{96,64},{0,96},{33,1},{65,33},{97,65},{1,97},{34,2}... | collective-permute-start | bytes 122888 | tf_op jit(solution)/shard_map/ppermute | solution.py:390
  25.0 6.8 %collective-permute-start.7 = (f32[5,40,128]{2,1,0:T(8,128)S(1)}, f32[5,40,128]{2,1,0:T(8,128)S(1)}, u32[]{:S(2)}, u32[]{:S(2)}) collective-permute-start(f32[5,40,128]{2,1,0:T(8,128)S(1)} %get-tuple-element.27), channel_id=1, source_target_pairs={{0,0},{1,2},{2,1},{3,4},{4,3},{5,6},{6,5},{7,8},{8,7},{9,10},{10,9... | collective-permute-start | bytes 307208 | tf_op jit(solution)/shard_map/ppermute | solution.py:416
  29.5 2.3 %collective-permute-start.6 = (f32[5,40,128]{2,1,0:T(8,128)S(1)}, f32[5,40,128]{2,1,0:T(8,128)S(1)}, u32[]{:S(2)}, u32[]{:S(2)}) collective-permute-start(f32[5,40,128]{2,1,0:T(8,128)S(1)} %get-tuple-element.28), channel_id=1, source_target_pairs={{0,1},{1,0},{2,3},{3,2},{4,5},{5,4},{6,7},{7,6},{8,9},{9,8},{10,11... | collective-permute-start | bytes 307208 | tf_op jit(solution)/shard_map/ppermute | solution.py:417

commit v6 on v5

--- a/solution.py
+++ b/solution.py
@@ -28,6 +28,7 @@
 HALO_ROWS = 40
 CHUNK = 4
 CHUNKS = XS // CHUNK
+FETCHES = ((0, 2), (2, 4)) + tuple((x, x + CHUNK) for x in range(4, XS, CHUNK))
 BLOCKS = 16
 BLOCK_ROWS = 19 * 32
 SLOT_ROWS = BLOCK_ROWS + 8
@@ -98,9 +99,9 @@
 def fetch(hbm, vmem, sem):
     return [
         pltpu.make_async_copy(
-            hbm.at[:, pl.ds(c * CHUNK, CHUNK)], vmem.at[:, pl.ds(1 + c * CHUNK, CHUNK)], sem.at[c]
+            hbm.at[:, pl.ds(low, high - low)], vmem.at[:, pl.ds(1 + low, high - low)], sem.at[c]
         )
-        for c in range(CHUNKS)
+        for c, (low, high) in enumerate(FETCHES)
     ]
 
 
@@ -186,10 +187,10 @@
         return carry
 
     copies[0].wait()
-    for c in range(CHUNKS):
-        if c + 1 < CHUNKS:
+    for c, (low, high) in enumerate(FETCHES):
+        if c + 1 < len(FETCHES):
             copies[c + 1].wait()
-        lax.fori_loop(c * CHUNK, (c + 1) * CHUNK, plane, 0, unroll=2)
+        lax.fori_loop(low, high, plane, 0, unroll=2)
     for k in range(5):
         xup[k] = out[X_UP[k], XS - 1]
         xdn[k] = out[X_DOWN[k], 0]
@@ -340,7 +341,7 @@
         out_specs=(VMEM,) * 5,
         scratch_shapes=[
             pltpu.VMEM((19, XS + 2, YS, ZS), jnp.float32),
-            pltpu.SemaphoreType.DMA((CHUNKS,)),
+            pltpu.SemaphoreType.DMA((len(FETCHES),)),
         ],
         compiler_params=params(),
         name="step_one",

time: 171 us -> 170 us (level)
  no operation moved by 1% of the time
where the time goes in v6:
time: 170 us
  blocking collectives  124 us (73%)
  Pallas kernels  21.7 us (13%)
  starting transfers between devices  16.2 us (10%)
  waiting for transfers between devices  6.44 us (4%)
    all_to_all x1, blocking collectives, per_device(): lax.all_to_all(outgoing, 'blk', split_axis=0, concat_axis=0, tiled=True)  124 us
    ppermute x2, starting transfers between devices, exchange(): outer = lax.ppermute(jnp.where(even, ydn, yup), 'blk', across)  9.69 us
    pallas_call x1, Pallas kernels, step_two(): pl.pallas_call(step_two_kernel, out_shape=sds(peers, SLOT_ROWS, ZS), in_s...  8.88 us
    ppermute x4, starting transfers between devices, shift(): return lax.ppermute(value, axis, steps)  6.3 us
    pallas_call x1, Pallas kernels, place(): pl.pallas_call(place_kernel, out_shape=sds(19, BLOCKS, 4096), in_specs=[A...  5.31 us
    pallas_call x1, Pallas kernels, step_one(): pl.pallas_call(step_one_kernel, out_shape=(sds(19, XS, YS, ZS), *EDGES),...  4.99 us
    ppermute x2, waiting for transfers between devices, exchange(): outer = lax.ppermute(jnp.where(even, ydn, yup), 'blk', across)  4.45 us
  transfers between devices with their start and end apart: 8, of which 4 were waited for; matrix products, arithmetic and copies ran while one was open for 0% of the time, Pallas kernels for 1%

profile of v6, /device:TPU:1, one launch (start us, length us, event | category | flops | bytes accessed | tf_op | source)
XLA Modules:
  0.0 170.1 jit_solution(14562819476982342490)
XLA Ops:
  0.0 0.0 copy-start
  0.0 0.8 fusion.12
  0.8 0.9 x_edges.1
  1.8 2.1 %collective-permute-start = (f32[5,16,128]{2,1,0:T(8,128)S(1)}, f32[5,16,128]{2,1,0:T(8,128)S(1)}, u32[]{:S(2)}, u32[]{:S(2)}) collective-permute-start(f32[5,16,128]{2,1,0:T(8,128)S(1)} %get-tuple-element.14), channel_id=1, source_target_pairs={{0,32},{32,64},{64,96},{96,0},{1,33},{33,65},{65,97},{97,1},{2,34}... | collective-permute-start | bytes 122888 | tf_op jit(solution)/shard_map/ppermute | solution.py:391
  3.9 1.3 collective-permute-start.1
  5.2 0.0 copy-done
  5.2 0.0 copy-done.1
  5.3 0.0 copy-start.2
  5.3 1.6 y_edges.1
  7.0 0.0 collective-permute-done.xlo
  7.0 0.0 collective-permute-done.1.xhi
  7.0 0.1 fusion.16
  7.1 0.1 fusion.17
  7.2 5.2 %collective-permute-start.3 = (f32[5,40,128]{2,1,0:T(8,128)S(1)}, f32[5,40,128]{2,1,0:T(8,128)S(1)}, u32[]{:S(2)}, u32[]{:S(2)}) collective-permute-start(f32[5,40,128]{2,1,0:T(8,128)S(1)} %get-tuple-element.29), channel_id=1, source_target_pairs={{0,0},{1,2},{2,1},{3,4},{4,3},{5,6},{6,5},{7,8},{8,7},{9,10},{10,9... | collective-permute-start | bytes 307208 | tf_op jit(solution)/shard_map/ppermute | solution.py:417
  12.5 0.1 collective-permute-start.2
  12.6 2.2 %collective-permute-done.3.outer = f32[5,40,128]{2,1,0:T(8,128)S(1)} collective-permute-done((f32[5,40,128]{2,1,0:T(8,128)S(1)}, f32[5,40,128]{2,1,0:T(8,128)S(1)}, u32[]{:S(2)}, u32[]{:S(2)}) %collective-permute-start.3) | collective-permute-done | bytes 102432 | tf_op jit(solution)/shard_map/ppermute | solution.py:417
  14.8 0.0 collective-permute-done.2.inner
  14.8 5.0 %step_one.1 = (f32[19,32,16,128]{3,2,1,0:T(8,128)S(1)}, f32[5,16,128]{2,1,0:T(8,128)S(1)}, f32[5,16,128]{2,1,0:T(8,128)S(1)}, f32[5,40,128]{2,1,0:T(8,128)S(1)}, f32[5,40,128]{2,1,0:T(8,128)S(1)}) custom-call(f32[19,32,16,128]{3,2,1,0:T(8,128)} %pops.5, f32[32,16,128]{2,1,0:T(8,128)S(1)} %select_select_fusion.mark, ...), custom_call_target="tpu_custom_call" | custom-call | tf_op jit(solution)/shard_map/step_one/pallas_call | solution.py:337
  19.8 1.3 collective-permute-start.4
  21.1 1.6 collective-permute-start.5
  22.7 1.4 collective-permute-done.4.xlo
  24.0 0.6 collective-permute-done.5.xhi
  24.6 0.1 fusion.15
  24.7 0.1 fusion.14
  24.8 4.4 %collective-permute-start.7 = (f32[5,40,128]{2,1,0:T(8,128)S(1)}, f32[5,40,128]{2,1,0:T(8,128)S(1)}, u32[]{:S(2)}, u32[]{:S(2)}) collective-permute-start(f32[5,40,128]{2,1,0:T(8,128)S(1)} %get-tuple-element.27), channel_id=1, source_target_pairs={{0,0},{1,2},{2,1},{3,4},{4,3},{5,6},{6,5},{7,8},{8,7},{9,10},{10,9... | collective-permute-start | bytes 307208 | tf_op jit(solution)/shard_map/ppermute | solution.py:417
  29.3 0.1 collective-permute-start.6
  29.4 0.0 copy-done.2
  29.4 2.2 %collective-permute-done.7.outer = f32[5,40,128]{2,1,0:T(8,128)S(1)} collective-permute-done((f32[5,40,128]{2,1,0:T(8,128)S(1)}, f32[5,40,128]{2,1,0:T(8,128)S(1)}, u32[]{:S(2)}, u32[]{:S(2)}) %collective-permute-start.7) | collective-permute-done | bytes 102432 | tf_op jit(solution)/shard_map/ppermute | solution.py:417
  31.6 0.0 collective-permute-done.6.inner
  31.6 8.9 %step_two.1 = f32[32,616,128]{2,1,0:T(8,128)} custom-call(s32[16]{0:T(128)S(1)} %and_select_fusion.owners, f32[19,32,16,128]{3,2,1,0:T(8,128)S(1)} %get-tuple-element.18.f, f32[5,16,128]{2,1,0:T(8,128)S(1)} %collective-permute-done.4.xlo, f32[5,16,128]{2,1,0:T(8,128)S(1)} %collective-permute-done.5.xhi, f32[5,40,128]{2,1,0:T(8,128)S(1)} %collective-permute-done.6.inner, ...), custom_call_target="tpu_custom_call" | custom-call | tf_op jit(solution)/shard_map/step_two/pallas_call | solution.py:352
  40.5 124.3 %all_to_all.5.incoming = f32[32,616,128]{2,1,0:T(8,128)} all-to-all(f32[32,616,128]{2,1,0:T(8,128)} %step_two.1), channel_id=1, replica_groups=mesh['slab'=4,'blk'=32] {'blk'}, dimensions={0} | all-to-all | bytes 20185088 | tf_op jit(solution)/shard_map/all_to_all | solution.py:442
  164.8 5.3 %place.1 = f32[19,16,4096]{2,1,0:T(8,128)} custom-call(f32[32,616,128]{2,1,0:T(8,128)} %all_to_all.5.incoming), custom_call_target="tpu_custom_call" | custom-call | tf_op jit(solution)/shard_map/place/pallas_call | solution.py:370
  (15 shorter events, 0.2 us)
Async XLA Ops:
  0.0 5.2 %copy-start = (s32[32,16,128]{2,1,0:T(8,128)S(1)}, s32[32,16,128]{2,1,0:T(8,128)}, u32[]{:S(2)}) copy-start(s32[32,16,128]{2,1,0:T(8,128)} %param.6) | copy-start | bytes 786436
  0.0 5.2 %copy-start.1 = (s32[32,16,128]{2,1,0:T(8,128)S(1)}, s32[32,16,128]{2,1,0:T(8,128)}, u32[]{:S(2)}) copy-start(s32[32,16,128]{2,1,0:T(8,128)} %param.5) | copy-start | bytes 786436
  1.8 5.2 %collective-permute-start = (f32[5,16,128]{2,1,0:T(8,128)S(1)}, f32[5,16,128]{2,1,0:T(8,128)S(1)}, u32[]{:S(2)}, u32[]{:S(2)}) collective-permute-start(f32[5,16,128]{2,1,0:T(8,128)S(1)} %get-tuple-element.14), channel_id=1, source_target_pairs={{0,32},{32,64},{64,96},{96,0},{1,33},{33,65},{65,97},{97,1},{2,34}... | collective-permute-start | bytes 122888 | tf_op jit(solution)/shard_map/ppermute | solution.py:391
  3.9 3.1 %collective-permute-start.1 = (f32[5,16,128]{2,1,0:T(8,128)S(1)}, f32[5,16,128]{2,1,0:T(8,128)S(1)}, u32[]{:S(2)}, u32[]{:S(2)}) collective-permute-start(f32[5,16,128]{2,1,0:T(8,128)S(1)} %get-tuple-element.15), channel_id=1, source_target_pairs={{32,0},{64,32},{96,64},{0,96},{33,1},{65,33},{97,65},{1,97},{34,2}... | collective-permute-start | bytes 122888 | tf_op jit(solution)/shard_map/ppermute | solution.py:391
  5.3 24.1 %copy-start.2 = (s32[1,16]{1,0:T(1,128)S(1)}, s32[1,16]{1,0:T(1,128)}, u32[]{:S(2)}) copy-start(s32[1,16]{1,0:T(1,128)} %param.7) | copy-start | bytes 196
  7.2 7.6 %collective-permute-start.3 = (f32[5,40,128]{2,1,0:T(8,128)S(1)}, f32[5,40,128]{2,1,0:T(8,128)S(1)}, u32[]{:S(2)}, u32[]{:S(2)}) collective-permute-start(f32[5,40,128]{2,1,0:T(8,128)S(1)} %get-tuple-element.29), channel_id=1, source_target_pairs={{0,0},{1,2},{2,1},{3,4},{4,3},{5,6},{6,5},{7,8},{8,7},{9,10},{10,9... | collective-permute-start | bytes 307208 | tf_op jit(solution)/shard_map/ppermute | solution.py:417
  12.5 2.3 %collective-permute-start.2 = (f32[5,40,128]{2,1,0:T(8,128)S(1)}, f32[5,40,128]{2,1,0:T(8,128)S(1)}, u32[]{:S(2)}, u32[]{:S(2)}) collective-permute-start(f32[5,40,128]{2,1,0:T(8,128)S(1)} %get-tuple-element.30), channel_id=1, source_target_pairs={{0,1},{1,0},{2,3},{3,2},{4,5},{5,4},{6,7},{7,6},{8,9},{9,8},{10,11... | collective-permute-start | bytes 307208 | tf_op jit(solution)/shard_map/ppermute | solution.py:418
  19.8 4.2 %collective-permute-start.4 = (f32[5,16,128]{2,1,0:T(8,128)S(1)}, f32[5,16,128]{2,1,0:T(8,128)S(1)}, u32[]{:S(2)}, u32[]{:S(2)}) collective-permute-start(f32[5,16,128]{2,1,0:T(8,128)S(1)} %get-tuple-element.19), channel_id=1, source_target_pairs={{0,32},{32,64},{64,96},{96,0},{1,33},{33,65},{65,97},{97,1},{2,34}... | collective-permute-start | bytes 122888 | tf_op jit(solution)/shard_map/ppermute | solution.py:391
  21.1 3.5 %collective-permute-start.5 = (f32[5,16,128]{2,1,0:T(8,128)S(1)}, f32[5,16,128]{2,1,0:T(8,128)S(1)}, u32[]{:S(2)}, u32[]{:S(2)}) collective-permute-start(f32[5,16,128]{2,1,0:T(8,128)S(1)} %get-tuple-element.20), channel_id=1, source_target_pairs={{32,0},{64,32},{96,64},{0,96},{33,1},{65,33},{97,65},{1,97},{34,2}... | collective-permute-start | bytes 122888 | tf_op jit(solution)/shard_map/ppermute | solution.py:391
  24.8 6.8 %collective-permute-start.7 = (f32[5,40,128]{2,1,0:T(8,128)S(1)}, f32[5,40,128]{2,1,0:T(8,128)S(1)}, u32[]{:S(2)}, u32[]{:S(2)}) collective-permute-start(f32[5,40,128]{2,1,0:T(8,128)S(1)} %get-tuple-element.27), channel_id=1, source_target_pairs={{0,0},{1,2},{2,1},{3,4},{4,3},{5,6},{6,5},{7,8},{8,7},{9,10},{10,9... | collective-permute-start | bytes 307208 | tf_op jit(solution)/shard_map/ppermute | solution.py:417
  29.3 2.3 %collective-permute-start.6 = (f32[5,40,128]{2,1,0:T(8,128)S(1)}, f32[5,40,128]{2,1,0:T(8,128)S(1)}, u32[]{:S(2)}, u32[]{:S(2)}) collective-permute-start(f32[5,40,128]{2,1,0:T(8,128)S(1)} %get-tuple-element.28), channel_id=1, source_target_pairs={{0,1},{1,0},{2,3},{3,2},{4,5},{5,4},{6,7},{7,6},{8,9},{9,8},{10,11... | collective-permute-start | bytes 307208 | tf_op jit(solution)/shard_map/ppermute | solution.py:418
